TPU v7x, 256 devices: a whole 4x4x8 slice. The times are simulated.
256 devices in a mesh: ctx: 32 (over y_hi, z, core), tp: 8 (over x, y_lo).
Axes of the slice: x: 4, y: 4 (y_hi: 2, y_lo: 2; y = y_hi * 2 + y_lo), z: 8, core: 2. Of those that a mesh axis runs over, the one named last changes fastest.
Arguments:
- student_rows: bfloat16 [8192, 8192], P('ctx', 'tp'), may hold values from -3 to 3
- queries: bfloat16 [8192, 4096], P('ctx', 'tp'), may hold values from -5 to 5
- keys_values: bfloat16 [2, 8192, 512], P(None, 'ctx'), may hold values from -5 to 5
- out_weight: bfloat16 [4096, 8192], P(None, 'tp'), may hold values from -0.09375 to 0.09375
- teacher_rows: bfloat16 [12288, 8192], P('ctx', 'tp'), may hold values from -6 to 6
- span_start: int32 [8192], P('ctx'), may hold values from 0 to 12287, as said below
- span_len: int32 [8192], P('ctx'), may hold values from 1 to 4, as said below
Outputs:
- student_out: bfloat16 [8192, 8192], P('ctx', 'tp')
- teacher_grad: bfloat16 [12288, 8192], P('ctx', 'tp')
Inputs may be any that keep to these rules, and one draw needn't show every extreme that they name: Student token s of shard c = s // 256 pools teacher tokens span_start[s] to span_start[s] + span_len[s] - 1, all within 8 tokens of shard c's block of teacher tokens c * 384 to (c + 1) * 384 - 1. The first student token of every shard but the first starts exactly 8 tokens before that block. `span_len`: the last student token of every shard but the last ends exactly 8 tokens after its shard's block.
All inputs are finite; a program needn't handle non-finite values.
Results may differ from a plain program's by a relative error of at most 0.012.
Values may be sent and summed in bfloat16 or wider, within the bound.
A program may use at most 128 MiB of HBM per device.

v0:
```python
import math

import jax
import jax.numpy as jnp
from jax import lax
from jax.sharding import Mesh
from jax.sharding import PartitionSpec as P

HEADS = 32
KVH = 4
HD = 128
HALO = 8
CTX = ("ctx_0", "ctx_1", "ctx_2")


floor_score = -1e30


def with_halo(array, sides, width):
    for axis, dim in sides:
        peers, length = (lax.axis_size(axis), array.shape[dim])
        up = [(i, (i + 1) % peers) for i in range(peers - 1)]
        down = [(j, i) for i, j in up]
        last = lax.slice_in_dim(array, length - width, length, axis=dim)
        leading = lax.slice_in_dim(array, 0, width, axis=dim)
        before = lax.ppermute(last, axis, up)
        after = lax.ppermute(leading, axis, down)
        array = jnp.concatenate([before, array, after], axis=dim)
    return array


def in_order(blocks, dim):
    shape = list(blocks.shape[1:])
    shape[dim] *= blocks.shape[0]
    return jnp.moveaxis(blocks, 0, dim).reshape(shape)


def stacked_from(array, axes, order):
    blocks = array
    for k in order:
        blocks = lax.all_gather(blocks, axes[k])
    done = order[::-1]
    back = [done.index(k) for k in range(len(axes))]
    blocks = blocks.transpose(*back, *range(len(axes), blocks.ndim))
    return blocks.reshape(-1, *array.shape)


def gathered_by_axis(array, axes, order, dim):
    return in_order(stacked_from(array, axes, order), dim)


def sent_to_all(array, axis):
    peers = lax.axis_size(axis)
    return lax.all_to_all(
        jnp.broadcast_to(array[None], (peers, *array.shape)), axis, 0, 0, tiled=True
    )


def collect(array, axis, dim):
    blocks = sent_to_all(array, axis)
    return in_order(blocks, dim)


def shifted(value, axis, steps):
    count = lax.axis_size(axis)
    leading, last = (max(0, -steps), min(count, count - steps))
    return lax.ppermute(value, axis, [(source, source + steps) for source in range(leading, last)])


def fresh_state(row_count, kv_count, per_kv, head_size):
    return (
        jnp.full((kv_count, per_kv, row_count), floor_score, jnp.float32),
        jnp.zeros((kv_count, per_kv, row_count), jnp.float32),
        jnp.zeros((kv_count, per_kv, row_count, head_size), jnp.float32),
    )


def attend(state, query_block, query_pos, key_rows, value_rows, key_pos):
    kv_count = query_block.shape[1]
    head_size = query_block.shape[3]
    score_scale = 1.0 / math.sqrt(head_size)
    key_heads = key_rows.reshape(key_rows.shape[0], kv_count, head_size)
    value_heads = value_rows.reshape(value_rows.shape[0], kv_count, head_size)

    def update(current):
        peak, total, accum = current
        scores = (
            jnp.einsum("rkgd,pkd->kgrp", query_block, key_heads, preferred_element_type=jnp.float32)
            * score_scale
        )
        visible = key_pos[None, :] <= query_pos[:, None]
        scores = jnp.where(visible, scores, floor_score)
        new_peak = jnp.maximum(peak, jnp.max(scores, axis=-1))
        weights = jnp.where(visible, jnp.exp(scores - new_peak[..., None]), 0.0)
        total = jnp.sum(weights, axis=-1)
        accum = jnp.einsum(
            "kgrp,pkd->kgrd",
            weights.astype(jnp.bfloat16),
            value_heads,
            preferred_element_type=jnp.float32,
        )
        return (new_peak, total, accum)

    def unchanged(current):
        return current

    return lax.cond(jnp.min(key_pos) > jnp.max(query_pos), unchanged, update, state)


def finish(state):
    peak, total, accum = state
    result = accum / total[..., None]
    return result.transpose(2, 0, 1, 3).reshape(result.shape[2], -1).astype(jnp.bfloat16)


def body(student_rows, queries, keys_values, out_weight, teacher_rows, span_start, span_len):
    ctx_rank = lax.axis_index(CTX)
    tp_lane = lax.axis_index("tp")
    rows_dev = student_rows.shape[0]
    teach_dev = teacher_rows.shape[0]
    heads_dev = queries.shape[1] // HD
    group_size = HEADS // KVH
    kv_dev = max(1, heads_dev // group_size)
    per_own = heads_dev // kv_dev
    extended = with_halo(teacher_rows, ((CTX, 0),), HALO)
    window = teach_dev + 2 * HALO
    columns = ctx_rank * teach_dev - HALO + jnp.arange(window)
    span_end = span_start + span_len
    member = (
        (columns[None, :] >= span_start[:, None]) & (columns[None, :] < span_end[:, None])
    ).astype(jnp.bfloat16)
    span_counts = span_len.astype(jnp.float32)[:, None]
    target = jnp.dot(member, extended, preferred_element_type=jnp.float32) / span_counts
    kv_first = tp_lane * heads_dev // group_size
    kv_own = lax.dynamic_slice_in_dim(keys_values, kv_first * HD, kv_dev * HD, 2)
    own_pos = ctx_rank * rows_dev + jnp.arange(rows_dev)
    block = queries.reshape(rows_dev, kv_dev, per_own, HD)
    initial = fresh_state(rows_dev, kv_dev, per_own, HD)
    piece = gathered_by_axis(kv_own, CTX, (0, 1, 2), 1)
    key_pos = jnp.arange(piece.shape[1])
    state = attend(initial, block, own_pos, piece[0], piece[1], key_pos)
    attended = finish(state)
    projected = jnp.dot(collect(attended, "tp", 1), out_weight, preferred_element_type=jnp.float32)
    student32 = student_rows.astype(jnp.float32) + projected
    resid = student32 - target
    weighted = (resid / span_counts).astype(jnp.bfloat16)
    spread = lax.dot_general(
        member, weighted, (((0,), (0,)), ((), ())), preferred_element_type=jnp.float32
    )
    from_above = shifted(spread[:HALO].astype(jnp.bfloat16), CTX, -1).astype(jnp.float32)
    from_below = shifted(spread[teach_dev + HALO :].astype(jnp.bfloat16), CTX, 1).astype(
        jnp.float32
    )
    core = spread[HALO : HALO + teach_dev]
    core = core.at[teach_dev - HALO :].add(from_above)
    core = core.at[:HALO].add(from_below)
    return (student32.astype(jnp.bfloat16), core.astype(jnp.bfloat16))


def solution(mesh):
    finer = Mesh(mesh.devices.reshape(2, 8, 2, mesh.shape["tp"]), ("ctx_0", "ctx_1", "ctx_2", "tp"))
    return jax.shard_map(
        body,
        mesh=finer,
        in_specs=(
            P(CTX, "tp"),
            P(CTX, "tp"),
            P(None, CTX, None),
            P(None, "tp"),
            P(CTX, "tp"),
            P(CTX),
            P(CTX),
        ),
        out_specs=(P(CTX, "tp"), P(CTX, "tp")),
        check_vma=False,
    )
```

profile of v0, /device:TPU:24, one launch (start us, length us, event | category | flops | bytes accessed | tf_op | source)
XLA Modules:
  0.0 200.8 jit_solution(9885638432147126324)
XLA Ops:
  7.2 1.0 copy-done
  8.2 7.5 %all-gather = bf16[4,256,128]{2,1,0:T(8,128)(2,1)} all-gather(bf16[2,256,128]{2,1,0:T(8,128)(2,1)S(1)} %constant_dynamic-slice_fusion), channel_id=2, replica_groups=mesh['ctx_0'=2,'ctx_1'=8,'ctx_2'=2,'tp'=8] {'ctx_0'}, dimensions={0}, use_global_device_ids=true | all-gather | bytes 393216 | tf_op jit(solution)/shard_map/all_gather | solution.py:41
  15.8 43.9 %all-gather.6.cloned.1.call-done = bf16[16,2,256,128]{3,2,1,0:T(8,128)(2,1)} async-done(((bf16[2,2,256,128]{3,2,1,0:T(8,128)(2,1)}), bf16[16,2,256,128]{3,2,1,0:T(8,128)(2,1)}) %all-gather.6.cloned.1.call-update) | async-done | bytes 2097168 | tf_op jit(solution)/shard_map/all_gather | solution.py:41
  61.1 18.1 %all-gather.8.cloned.1.call-done = bf16[16,2,2,256,128]{4,3,2,1,0:T(8,128)(2,1)} async-done(((bf16[8,2,2,256,128]{4,3,2,1,0:T(8,128)(2,1)}), bf16[16,2,2,256,128]{4,3,2,1,0:T(8,128)(2,1)}) %all-gather.8.cloned.1.call-update) | async-done | bytes 4194320 | tf_op jit(solution)/shard_map/all_gather | solution.py:41
  79.1 2.5 %copy.22 = bf16[2,8,2,2,256,128]{5,4,3,2,1,0:T(8,128)(2,1)S(1)} copy(bf16[2,8,2,2,256,128]{5,4,3,0,1,2:T(8,128)(2,1)} %bitcast.62) | data formatting | bytes 8388608 | tf_op jit(solution)/shard_map/transpose | solution.py:44
  81.7 48.8 %conditional.1 = (f32[1,4,256]{2,1,0:T(4,128)S(1)}, f32[1,4,256,128]{2,3,1,0:T(8,128)S(1)}) conditional(s32[]{:T(128)} %convert_element_type.44, (s32[8192]{0:T(1024)S(1)}, s32[256]{0:T(256)S(1)}, bf16[2,32,256,128]{3,2,0,1:T(8,128)(2,1)S(1)}, bf16[256,512]{1,0:T(8,128)(2,1)S(1)}) %tuple.46, () %tuple.25), branch_computations={%region_1.0_spmd, %region_4.5_spmd} | conditional | flops 4406115328 | bytes 122479632 | solution.py:107
  81.7 3.7 %broadcast_compare_fusion = pred[256,8192]{0,1:T(8,128)(4,1)S(1)} fusion(s32[256]{0:T(256)S(1)} %get-tuple-element.39, s32[8192]{0:T(1024)S(1)} %get-tuple-element.38), kind=kLoop, calls=%fused_computation.8 | loop fusion | flops 2097152 | bytes 2130944 | tf_op jit(solution)/shard_map/cond/branch_0_fun/le | solution.py:91
  85.4 1.6 fusion.48
  87.0 13.5 %fusion = (f32[4,256]{1,0:T(4,128)S(1)}, f32[8192,256,4]{1,0,2:T(8,128)}) fusion(pred[256,8192]{0,1:T(8,128)(4,1)S(1)} %broadcast_compare_fusion, bf16[8192,128,1]{1,0,2:T(8,128)(2,1)S(1)} %bitcast.65, bf16[256,512]{1,0:T(8,128)(2,1)S(1)} %get-tuple-element.49), kind=kOutput, calls=%fused_computation.2 | convolution fusion | flops 2172648448 | bytes 38014976 | tf_op jit(solution)/shard_map/cond/branch_0_fun/rkgd,pkd->kgrp/dot_general | solution.py:88
  100.5 14.9 %fusion.7 = f32[1,4,256,128]{2,3,1,0:T(8,128)S(1)} fusion(bf16[8192,128,1]{1,0,2:T(8,128)(2,1)} %bitcast.64, f32[8192,256,4]{1,0,2:T(8,128)} %get-tuple-element.62, f32[4,256]{1,0:T(4,128)S(1)} %broadcast_maximum_fusion, pred[256,8192]{0,1:T(8,128)(4,1)S(1)} %broadcast_compare_fusion), kind=kOutput, calls=%fused_computation.9 | convolution fusion | flops 2189426688 | bytes 38277120 | tf_op jit(solution)/shard_map/cond/branch_0_fun/kgrp,pkd->kgrd/dot_general | solution.py:96
  115.4 15.0 %fusion.2 = f32[4,256]{1,0:T(4,128)S(1)} fusion(f32[8192,256,4]{1,0,2:T(8,128)} %get-tuple-element.62, f32[4,256]{1,0:T(4,128)S(1)} %broadcast_maximum_fusion, pred[256,8192]{0,1:T(8,128)(4,1)S(1)} %broadcast_compare_fusion), kind=kLoop, calls=%fused_computation.4 | loop fusion | flops 41942016 | bytes 35659776 | tf_op jit(solution)/shard_map/cond/branch_0_fun/reduce_sum | solution.py:95
  130.5 0.7 copy-done.3
  131.2 1.1 divide_convert_fusion
  132.3 1.5 broadcast_in_dim.36
  133.8 5.7 %all-to-all-start = ((bf16[8,256,512]{1,2,0:T(8,128)(2,1)}), bf16[8,256,512]{1,2,0:T(8,128)(2,1)S(1)}, u32[]{:S(2)}, u32[]{:S(2)}) async-start(bf16[8,256,512]{1,2,0:T(8,128)(2,1)} %broadcast_in_dim.36), calls=%async_computation | async-start | bytes 4194304 | tf_op jit(solution)/shard_map/all_to_all | solution.py:54
  140.2 1.9 collective-permute-start
  142.2 7.4 %collective-permute-start.1 = (bf16[8,1024]{1,0:T(8,128)(2,1)S(1)}, bf16[8,1024]{1,0:T(8,128)(2,1)S(1)}, u32[]{:S(2)}, u32[]{:S(2)}) collective-permute-start(bf16[8,1024]{1,0:T(8,128)(2,1)S(1)} %get-tuple-element.66), channel_id=1, source_target_pairs={{8,0},{16,8},{24,16},{32,24},{40,32},{48,40},{56,48},{64,56},{72,6... | collective-permute-start | bytes 49160 | tf_op jit(solution)/shard_map/ppermute | solution.py:27
  149.7 20.5 %all-to-all-done = bf16[8,256,512]{1,2,0:T(8,128)(2,1)S(1)} async-done(((bf16[8,256,512]{1,2,0:T(8,128)(2,1)}), bf16[8,256,512]{1,2,0:T(8,128)(2,1)S(1)}, u32[]{:S(2)}, u32[]{:S(2)}) %all-to-all-start) | async-done | bytes 2097184 | tf_op jit(solution)/shard_map/all_to_all | solution.py:54
  170.1 6.9 %fusion.52 = (bf16[256,1024]{1,0:T(8,128)(2,1)}, f32[256,1024]{1,0:T(8,128)}) fusion(bf16[256,4096]{0,1:T(8,128)(2,1)S(1)} %bitcast.61, bf16[4096,1024]{1,0:T(8,128)(2,1)} %param.16, bf16[256,1024]{1,0:T(8,128)(2,1)S(1)} %copy-done.2), kind=kOutput, calls=%fused_computation.49 | convolution fusion | flops 2148270080 | bytes 12582912 | tf_op jit(solution)/shard_map/dot_general | solution.py:143
  177.0 2.3 %fusion.53 = (bf16[400,1024]{1,0:T(8,128)(2,1)S(1)}, f32[400,1024]{1,0:T(8,128)S(1)}) fusion(f32[256,1024]{1,0:T(8,128)} %get-tuple-element.70, bf16[8,1024]{1,0:T(8,128)(2,1)S(1)} %collective-permute-done.1, bf16[384,1024]{1,0:T(8,128)(2,1)} %param.17, bf16[8,1024]{1,0:T(8,128)(2,1)S(1)} %collective-permute-done, f32[256]{0:T(256)S(1)} %get-tuple-element.68, ...), kind=kOutput, calls=%fused_computation.50 | convolution fusion | flops 423960576 | bytes 4330048 | tf_op jit(solution)/shard_map/dot_general | solution.py:147
  179.3 4.8 %collective-permute-start.2 = (bf16[8,1024]{1,0:T(8,128)(2,1)S(1)}, bf16[8,1024]{1,0:T(8,128)(2,1)S(1)}, u32[]{:S(2)}, u32[]{:S(2)}) collective-permute-start(bf16[8,1024]{1,0:T(8,128)(2,1)S(1)} %get-tuple-element.64), channel_id=1, source_target_pairs={{8,0},{16,8},{24,16},{32,24},{40,32},{48,40},{56,48},{64,56},{72,6... | collective-permute-start | bytes 49160 | tf_op jit(solution)/shard_map/ppermute | solution.py:67
  184.3 1.9 collective-permute-start.3
  186.3 6.7 %collective-permute-done.3 = bf16[8,1024]{1,0:T(8,128)(2,1)S(1)} collective-permute-done((bf16[8,1024]{1,0:T(8,128)(2,1)S(1)}, bf16[8,1024]{1,0:T(8,128)(2,1)S(1)}, u32[]{:S(2)}, u32[]{:S(2)}) %collective-permute-start.3) | collective-permute-done | bytes 16416 | tf_op jit(solution)/shard_map/ppermute | solution.py:67
  193.0 1.0 convert_element_type.53
  (30 shorter events, 1.8 us)
Async XLA Ops:
  7.2 1.1 copy-start
  7.2 52.6 %all-gather.6.cloned.1.call-start = ((), (), s32[]{:S(2)}) async-start(), calls=%async_computation.1 | async-start | bytes 2359296 | tf_op jit(solution)/shard_map/all_gather | solution.py:41
  15.8 63.3 %all-gather.8.cloned.1.call-start = ((), (), s32[]{:S(2)}) async-start(), calls=%async_computation.2 | async-start | bytes 6291456 | tf_op jit(solution)/shard_map/all_gather | solution.py:41
  79.1 2.5 %copy-start.6 = (bf16[256,512]{1,0:T(8,128)(2,1)S(1)}, bf16[256,512]{1,0:T(8,128)(2,1)}, u32[]{:S(2)}) copy-start(bf16[256,512]{1,0:T(8,128)(2,1)} %param.14) | copy-start | bytes 786436
  130.4 0.8 copy-start.3
  130.4 19.2 %copy-start.4 = (s32[256]{0:T(256)S(1)}, s32[256]{0:T(256)}, u32[]{:S(2)}) copy-start(s32[256]{0:T(256)} %param.19) | copy-start | bytes 3076
  130.5 19.2 %copy-start.5 = (s32[256]{0:T(256)S(1)}, s32[256]{0:T(256)}, u32[]{:S(2)}) copy-start(s32[256]{0:T(256)} %param.18) | copy-start | bytes 3076
  130.5 39.6 %copy-start.2 = (bf16[256,1024]{1,0:T(8,128)(2,1)S(1)}, bf16[256,1024]{1,0:T(8,128)(2,1)}, u32[]{:S(2)}) copy-start(bf16[256,1024]{1,0:T(8,128)(2,1)} %param.13) | copy-start | bytes 1572868
  133.8 36.3 %all-to-all-start = ((bf16[8,256,512]{1,2,0:T(8,128)(2,1)}), bf16[8,256,512]{1,2,0:T(8,128)(2,1)S(1)}, u32[]{:S(2)}, u32[]{:S(2)}) async-start(bf16[8,256,512]{1,2,0:T(8,128)(2,1)} %broadcast_in_dim.36), calls=%async_computation | async-start | bytes 4194304 | tf_op jit(solution)/shard_map/all_to_all | solution.py:54
  140.2 36.7 %collective-permute-start = (bf16[8,1024]{1,0:T(8,128)(2,1)S(1)}, bf16[8,1024]{1,0:T(8,128)(2,1)S(1)}, u32[]{:S(2)}, u32[]{:S(2)}) collective-permute-start(bf16[8,1024]{1,0:T(8,128)(2,1)S(1)} %get-tuple-element.65), channel_id=1, source_target_pairs={{0,8},{8,16},{16,24},{24,32},{32,40},{40,48},{48,56},{56,64},{64,7... | collective-permute-start | bytes 49160 | tf_op jit(solution)/shard_map/ppermute | solution.py:26
  142.2 34.8 %collective-permute-start.1 = (bf16[8,1024]{1,0:T(8,128)(2,1)S(1)}, bf16[8,1024]{1,0:T(8,128)(2,1)S(1)}, u32[]{:S(2)}, u32[]{:S(2)}) collective-permute-start(bf16[8,1024]{1,0:T(8,128)(2,1)S(1)} %get-tuple-element.66), channel_id=1, source_target_pairs={{8,0},{16,8},{24,16},{32,24},{40,32},{48,40},{56,48},{64,56},{72,6... | collective-permute-start | bytes 49160 | tf_op jit(solution)/shard_map/ppermute | solution.py:27
  177.0 17.0 %copy-start.1 = (bf16[2,256,512]{2,1,0:T(8,128)(2,1)S(1)}, bf16[2,256,512]{2,1,0:T(8,128)(2,1)}, u32[]{:S(2)}) copy-start(bf16[2,256,512]{2,1,0:T(8,128)(2,1)} %param.15) | copy-start | bytes 1572868
  179.3 7.0 %collective-permute-start.2 = (bf16[8,1024]{1,0:T(8,128)(2,1)S(1)}, bf16[8,1024]{1,0:T(8,128)(2,1)S(1)}, u32[]{:S(2)}, u32[]{:S(2)}) collective-permute-start(bf16[8,1024]{1,0:T(8,128)(2,1)S(1)} %get-tuple-element.64), channel_id=1, source_target_pairs={{8,0},{16,8},{24,16},{32,24},{40,32},{48,40},{56,48},{64,56},{72,6... | collective-permute-start | bytes 49160 | tf_op jit(solution)/shard_map/ppermute | solution.py:67
  184.3 8.7 %collective-permute-start.3 = (bf16[8,1024]{1,0:T(8,128)(2,1)S(1)}, bf16[8,1024]{1,0:T(8,128)(2,1)S(1)}, u32[]{:S(2)}, u32[]{:S(2)}) collective-permute-start(bf16[8,1024]{1,0:T(8,128)(2,1)S(1)} %get-tuple-element.63), channel_id=1, source_target_pairs={{0,8},{8,16},{16,24},{24,32},{32,40},{40,48},{48,56},{56,64},{64,7... | collective-permute-start | bytes 49160 | tf_op jit(solution)/shard_map/ppermute | solution.py:67
Sparse Core Ops, SparseCore 0:
  15.9 43.8 all-gather.5
  61.5 17.5 all-gather.7
where the time goes:
time: 201 us
  waiting for transfers between devices  89.2 us (44%)
  matrix products  37.6 us (19%)
  starting transfers between devices  21.9 us (11%)
  other arithmetic  21.5 us (11%)
  between operations  14.9 us (7%)
  local copies, waits for them, and re-layouts  8.24 us (4%)
  blocking collectives  7.52 us (4%)
    all_gather x2, waiting for transfers between devices, stacked_from(): blocks = lax.all_gather(blocks, axes[k])  62 us
    all_to_all x1, waiting for transfers between devices, sent_to_all(): lax.all_to_all(jnp.broadcast_to(array[None], (peers, *array.shape)), axis...  20.5 us
    reduce_sum x1, other arithmetic, update(): total = jnp.sum(weights, axis=-1)  15 us
    dot_general x1, matrix products, update(): jnp.einsum('kgrp,pkd->kgrd', weights.astype(jnp.bfloat16), value_heads, p...  14.9 us
    dot_general x1, matrix products, update(): jnp.einsum('rkgd,pkd->kgrp', query_block, key_heads, preferred_element_ty...  13.5 us
    all_gather x1, blocking collectives, stacked_from(): blocks = lax.all_gather(blocks, axes[k])  7.52 us
    ppermute x1, starting transfers between devices, with_halo(): after = lax.ppermute(leading, axis, down)  7.44 us
    dot_general x1, matrix products, body(): jnp.dot(collect(attended, 'tp', 1), out_weight, preferred_element_type=jn...  6.88 us
  transfers between devices with their start and end apart: 7, of which 4 were waited for; matrix products, arithmetic and copies ran while one was open for 4% of the time, Pallas kernels for 0%

commit v1 on v0

v1 whole, which is shorter than its diff:
```python
import functools
import math

import jax
import jax.numpy as jnp
from jax import lax
from jax.experimental import pallas as pl
from jax.experimental.pallas import tpu as pltpu
from jax.sharding import PartitionSpec as P

HD = 128
S_DEV = 256
HALO = 8
N_Z = 8
MESH = pl.DeviceIdType.MESH
EXP_SCALE = math.log2(math.e) / math.sqrt(HD)
LOW = -1e30


def pick(step, table):
    value = table[0]
    for k in range(1, len(table)):
        value = jnp.where(step == k, table[k], value)
    return value


def attend_kernel(
    q_ref, kv_ref, out_ref, buf, own_v, q_t, scores, peak, decay, total, accum,
    recv, send_right, send_left, send_sib, send_cross, send_pair, load,
):
    ctx, tp = lax.axis_index("ctx"), lax.axis_index("tp")
    core, z, y_hi = ctx % 2, (ctx // 2) % N_Z, ctx // 16
    x, y_lo = tp // 2, tp % 2
    sibling = ctx + 1 - 2 * core
    right = y_hi * 16 + ((z + 1) % N_Z) * 2 + core
    left = y_hi * 16 + ((z + N_Z - 1) % N_Z) * 2 + core
    other_hi = (ctx + 16) % 32
    pair = tp + 1 - 2 * y_lo
    kind_in, kind_swap = 1 - y_lo, y_lo

    def at(hi, steps):
        return hi * 16 + ((z + steps + N_Z) % N_Z) * 2 + core

    def swap(slot):
        return slot + 1 - 2 * core

    def part(kind, slot):
        return buf.at[kind, pl.ds(pl.multiple_of(slot * S_DEV, S_DEV), S_DEV)]

    def copy(kind, slot, to_ctx, to_tp, sem):
        return pltpu.make_async_remote_copy(
            src_ref=part(kind, slot), dst_ref=part(kind, slot), send_sem=sem,
            recv_sem=recv.at[kind, slot], device_id=(to_ctx, to_tp), device_id_type=MESH,
        )

    def arrived(kind, slot):
        copy(kind, slot, sibling, tp, send_sib.at[kind, slot]).wait_recv()

    def to_sibling(kind, slot):
        return copy(kind, slot, sibling, tp, send_sib.at[kind, slot])

    def to_right(kind, hops):
        return copy(kind, at(y_hi, -hops), right, tp, send_right.at[kind, hops])

    def to_left(kind, hops):
        return copy(kind, at(y_hi, hops), left, tp, send_left.at[kind, hops])

    def to_cross(slot):
        return copy(y_lo, slot, other_hi, pair, send_cross.at[slot // 2 % N_Z])

    def to_pair(slot):
        return copy(kind_in, slot, ctx, pair, send_pair.at[slot // 2 % N_Z])

    k_load = pltpu.make_async_copy(
        kv_ref.at[0, :, pl.ds(pl.multiple_of(x * HD, HD), HD)], part(0, ctx), load.at[0]
    )
    v_load = pltpu.make_async_copy(
        kv_ref.at[1, :, pl.ds(pl.multiple_of(x * HD, HD), HD)], own_v, load.at[1]
    )
    k_load.start()
    v_load.start()
    barrier = pltpu.get_barrier_semaphore()
    for to_ctx, to_tp in (
        (right, tp), (left, tp), (sibling, tp), (other_hi, pair), (ctx, pair),
    ):
        pl.semaphore_signal(barrier, inc=1, device_id=(to_ctx, to_tp), device_id_type=MESH)
    v_load.wait()
    v_own = own_v[...].astype(jnp.float32)
    for half in range(2):
        turned = v_own[half * HD : (half + 1) * HD].T.astype(jnp.bfloat16)
        start = pl.multiple_of(ctx * S_DEV + half * HD, HD)
        buf[1, pl.ds(start, HD), :] = turned
    k_load.wait()
    pl.semaphore_wait(barrier, 5)

    for kind in range(2):
        to_sibling(kind, ctx).start()
        to_right(kind, 0).start()
        to_left(kind, 0).start()

    @pl.when(y_hi == 0)
    def _():
        to_cross(ctx).start()

    for h in range(4):
        q_t[:, h * S_DEV : (h + 1) * S_DEV] = (
            q_ref[:, h * HD : (h + 1) * HD].astype(jnp.float32).T.astype(jnp.bfloat16)
        )

    def ring(hops):
        def side(kind, moving_right):
            slot = at(y_hi, -hops if moving_right else hops)
            arrived(kind, slot)
            last = 3 if (kind == 0) == moving_right else 2
            if hops <= last:
                (to_right if moving_right else to_left)(kind, hops).start()
            to_sibling(kind, slot).start()

            @pl.when((y_hi == 0) & (y_lo == kind))
            def _():
                to_cross(slot).start()

        if hops < 4:
            for kind in range(2):
                side(kind, True)
                side(kind, False)
        else:
            side(0, True)
            side(1, False)

    def low_slots(hops):
        if hops in (0, 4):
            return [at(0, hops)]
        return [at(0, -hops), at(0, hops)]

    def from_cross(hops):
        for slot in low_slots(hops):
            arrived(kind_in, slot)
            to_pair(slot).start()
            to_sibling(kind_in, slot).start()

    def from_pair(hops):
        for slot in low_slots(hops):
            arrived(kind_swap, slot)
            to_sibling(kind_swap, slot).start()

    half_rows = 2 * S_DEV

    def score(block, c, masked=False):
        cols = slice(c * half_rows, (c + 1) * half_rows)
        keys = buf[0, pl.ds(pl.multiple_of(block * 2 * S_DEV, 2 * S_DEV), 2 * S_DEV), :]
        s = jnp.dot(keys, q_t[:, cols], preferred_element_type=jnp.float32)
        if masked:
            key_pos = lax.broadcasted_iota(jnp.int32, s.shape, 0)
            query_pos = lax.broadcasted_iota(jnp.int32, s.shape, 1) % S_DEV + core * S_DEV
            s = jnp.where(key_pos <= query_pos, s, LOW)
        scores[c] = s
        new_peak = jnp.max(s, axis=0, keepdims=True)
        if not masked:
            old = peak[:, cols]
            new_peak = jnp.maximum(old, new_peak)
            decay[:, cols] = jnp.exp2((old - new_peak) * EXP_SCALE)
        peak[:, cols] = new_peak

    def gather_values(block, c, first=False):
        cols = slice(c * half_rows, (c + 1) * half_rows)
        weights = jnp.exp2((scores[c] - peak[:, cols]) * EXP_SCALE)
        added = jnp.sum(weights, axis=0, keepdims=True)
        rounded = weights.astype(jnp.bfloat16)
        base = block * 2 * S_DEV
        product = None
        for k in range(2):
            parts = [
                buf[1, pl.ds(pl.multiple_of(base + k * S_DEV + g * HD, HD), HD), :]
                for g in range(2)
            ]
            values = jnp.concatenate(parts, axis=1)
            term = jnp.dot(
                values, rounded[k * S_DEV : (k + 1) * S_DEV], preferred_element_type=jnp.float32
            )
            product = term if product is None else product + term
        if first:
            total[:, cols] = added
            accum[:, cols] = product
        else:
            shrink = decay[:, cols]
            total[:, cols] = total[:, cols] * shrink + added
            accum[:, cols] = accum[:, cols] * shrink + product

    own_block = ctx // 2
    for kind in range(2):
        arrived(kind, sibling)
    score(own_block, 0, masked=True)
    score(own_block, 1, masked=True)
    gather_values(own_block, 0, first=True)
    total[:, half_rows:] = jnp.zeros((1, half_rows), jnp.float32)
    accum[:, half_rows:] = jnp.zeros((HD, half_rows), jnp.float32)
    decay[:, half_rows:] = jnp.ones((1, half_rows), jnp.float32)

    events = {
        1: [(ring, 1)], 2: [(from_cross, 0)], 3: [(ring, 2), (from_pair, 0)],
        4: [(from_cross, 1)], 5: [(from_pair, 1)], 6: [(ring, 3), (from_cross, 2)],
        7: [(from_pair, 2)], 9: [(ring, 4), (from_cross, 3)], 10: [(from_pair, 3)],
        12: [(from_cross, 4)], 13: [(from_pair, 4)],
    }
    order = [
        None, ("own", -1), ("own", 1), ("own", -2), ("low", 0), ("own", 2), ("low", -1), ("own", -3),
        ("low", 1), ("own", 3), ("low", -2), ("own", 4), ("low", 2), ("low", -3), ("low", 3), ("low", 4),
    ]
    is_low = [0] + [1 if kind == "low" else 0 for kind, _ in order[1:]]
    shift = [0] + [steps for _, steps in order[1:]]

    def step(n, before):
        low = pick(n, is_low)
        block_z = (z + pick(n, shift) + N_Z) % N_Z
        for k, todo in events.items():
            for action, hops in todo:
                when = n == k
                if action is not ring:
                    when = when & (y_hi == 1)

                @pl.when(when)
                def _(action=action, hops=hops):
                    action(hops)

        block = jnp.where(low == 1, block_z, y_hi * N_Z + block_z)
        here = (low == 0) | (y_hi == 1)

        @pl.when(here)
        def _():
            for kind in range(2):
                arrived(kind, block * 2 + 1 - core)

        def compute(prior):
            score(block, 0)
            gather_values(prior, 1)
            score(block, 1)
            gather_values(block, 0)
            return block

        return lax.cond(here & (block < own_block), compute, lambda prior: prior, before)

    last_block = lax.fori_loop(1, 16, step, own_block)
    gather_values(last_block, 1)
    for h in range(4):
        cols = slice(h * S_DEV, (h + 1) * S_DEV)
        out_ref[:, h * HD : (h + 1) * HD] = (accum[:, cols] / total[:, cols]).T.astype(jnp.bfloat16)

    for kind in range(2):
        for hops in range(4 if kind == 0 else 3):
            to_right(kind, hops).wait_send()
        for hops in range(3 if kind == 0 else 4):
            to_left(kind, hops).wait_send()

    def sent(slot, _):
        for kind in range(2):
            to_sibling(kind, y_hi * 16 + slot * 2 + core).wait_send()

        @pl.when(y_hi == 0)
        def _():
            to_cross(slot * 2 + core).wait_send()

        @pl.when(y_hi == 1)
        def _():
            to_pair(slot * 2 + core).wait_send()
            for kind in range(2):
                to_sibling(kind, slot * 2 + core).wait_send()

        return 0

    lax.fori_loop(0, N_Z, sent, 0)


def attention(queries, keys_values):
    rows = queries.shape[0]
    wide = 4 * rows
    return pl.pallas_call(
        attend_kernel,
        out_shape=jax.ShapeDtypeStruct(queries.shape, jnp.bfloat16),
        in_specs=[pl.BlockSpec(memory_space=pltpu.VMEM), pl.BlockSpec(memory_space=pl.ANY)],
        out_specs=pl.BlockSpec(memory_space=pltpu.VMEM),
        scratch_shapes=[
            pltpu.VMEM((2, 32 * S_DEV, HD), jnp.bfloat16),
            pltpu.VMEM((S_DEV, HD), jnp.bfloat16),
            pltpu.VMEM((HD, wide), jnp.bfloat16),
            pltpu.VMEM((2, 2 * S_DEV, wide // 2), jnp.float32),
            pltpu.VMEM((1, wide), jnp.float32),
            pltpu.VMEM((1, wide), jnp.float32),
            pltpu.VMEM((1, wide), jnp.float32),
            pltpu.VMEM((HD, wide), jnp.float32),
            pltpu.SemaphoreType.DMA((2, 32)),
            pltpu.SemaphoreType.DMA((2, 4)),
            pltpu.SemaphoreType.DMA((2, 4)),
            pltpu.SemaphoreType.DMA((2, 32)),
            pltpu.SemaphoreType.DMA((N_Z,)),
            pltpu.SemaphoreType.DMA((N_Z,)),
            pltpu.SemaphoreType.DMA((2,)),
        ],
        compiler_params=pltpu.CompilerParams(
            collective_id=0, has_side_effects=True, vmem_limit_bytes=40 << 20
        ),
        name="attention",
    )(queries, keys_values)


def with_halo(array, sides, width):
    for axis, dim in sides:
        peers, length = (lax.axis_size(axis), array.shape[dim])
        up = [(i, (i + 1) % peers) for i in range(peers - 1)]
        down = [(j, i) for i, j in up]
        last = lax.slice_in_dim(array, length - width, length, axis=dim)
        leading = lax.slice_in_dim(array, 0, width, axis=dim)
        before = lax.ppermute(last, axis, up)
        after = lax.ppermute(leading, axis, down)
        array = jnp.concatenate([before, array, after], axis=dim)
    return array


def in_order(blocks, dim):
    shape = list(blocks.shape[1:])
    shape[dim] *= blocks.shape[0]
    return jnp.moveaxis(blocks, 0, dim).reshape(shape)


def sent_to_all(array, axis):
    peers = lax.axis_size(axis)
    return lax.all_to_all(
        jnp.broadcast_to(array[None], (peers, *array.shape)), axis, 0, 0, tiled=True
    )


def collect(array, axis, dim):
    blocks = sent_to_all(array, axis)
    return in_order(blocks, dim)


def shifted(value, axis, steps):
    count = lax.axis_size(axis)
    leading, last = (max(0, -steps), min(count, count - steps))
    return lax.ppermute(value, axis, [(source, source + steps) for source in range(leading, last)])


def body(student_rows, queries, keys_values, out_weight, teacher_rows, span_start, span_len):
    ctx_rank = lax.axis_index("ctx")
    teach_dev = teacher_rows.shape[0]
    extended = with_halo(teacher_rows, (("ctx", 0),), HALO)
    window = teach_dev + 2 * HALO
    columns = ctx_rank * teach_dev - HALO + jnp.arange(window)
    span_end = span_start + span_len
    member = (
        (columns[None, :] >= span_start[:, None]) & (columns[None, :] < span_end[:, None])
    ).astype(jnp.bfloat16)
    span_counts = span_len.astype(jnp.float32)[:, None]
    target = jnp.dot(member, extended, preferred_element_type=jnp.float32) / span_counts
    attended = attention(queries, keys_values)
    projected = jnp.dot(collect(attended, "tp", 1), out_weight, preferred_element_type=jnp.float32)
    student32 = student_rows.astype(jnp.float32) + projected
    resid = student32 - target
    weighted = (resid / span_counts).astype(jnp.bfloat16)
    spread = lax.dot_general(
        member, weighted, (((0,), (0,)), ((), ())), preferred_element_type=jnp.float32
    )
    from_above = shifted(spread[:HALO].astype(jnp.bfloat16), "ctx", -1).astype(jnp.float32)
    from_below = shifted(spread[teach_dev + HALO :].astype(jnp.bfloat16), "ctx", 1).astype(
        jnp.float32
    )
    core = spread[HALO : HALO + teach_dev]
    core = core.at[teach_dev - HALO :].add(from_above)
    core = core.at[:HALO].add(from_below)
    return (student32.astype(jnp.bfloat16), core.astype(jnp.bfloat16))


def solution(mesh):
    return jax.shard_map(
        body,
        mesh=mesh,
        in_specs=(
            P("ctx", "tp"),
            P("ctx", "tp"),
            P(None, "ctx", None),
            P(None, "tp"),
            P("ctx", "tp"),
            P("ctx"),
            P("ctx"),
        ),
        out_specs=(P("ctx", "tp"), P("ctx", "tp")),
        check_vma=False,
    )
```

time: 201 us -> 101 us (0.50)
  the two profiles are of different devices: /device:TPU:24 before, /device:TPU:16 now
where the time goes in v1:
time: 101 us; the launch traced here: 100 us
  Pallas kernels  38.6 us (38%)
  waiting for transfers between devices  26.4 us (26%)
  starting transfers between devices  18.6 us (18%)
  matrix products  9.41 us (9%)
  local copies, waits for them, and re-layouts  5.24 us (5%)
  other arithmetic  1.02 us (1%)
    pallas_call x1, Pallas kernels, attention(): pl.pallas_call(attend_kernel, out_shape=jax.ShapeDtypeStruct(queries.shap...  38.6 us
    all_to_all x1, waiting for transfers between devices, sent_to_all(): lax.all_to_all(jnp.broadcast_to(array[None], (peers, *array.shape)), axis...  20.3 us
    ppermute x1, starting transfers between devices, with_halo(): after = lax.ppermute(leading, axis, down)  7.26 us
    dot_general x1, matrix products, body(): jnp.dot(collect(attended, 'tp', 1), out_weight, preferred_element_type=jn...  6.58 us
    ppermute x2, waiting for transfers between devices, shifted(): lax.ppermute(value, axis, [(source, source + steps) for source in range(l...  6.06 us
    all_to_all x1, starting transfers between devices, sent_to_all(): lax.all_to_all(jnp.broadcast_to(array[None], (peers, *array.shape)), axis...  5.14 us
    ppermute x2, starting transfers between devices, shifted(): lax.ppermute(value, axis, [(source, source + steps) for source in range(l...  4.31 us
    dot_general x1, matrix products, body(): lax.dot_general(member, weighted, (((0,), (0,)), ((), ())), preferred_ele...  2.82 us
  transfers between devices with their start and end apart: 5, of which 2 were waited for; matrix products, arithmetic and copies ran while one was open for 7% of the time, Pallas kernels for 0%

profile of v1, /device:TPU:16, one launch (start us, length us, event | category | flops | bytes accessed | tf_op | source)
XLA Modules:
  0.0 100.1 jit_solution(10021155872116881741)
XLA Ops:
  0.6 0.0 copy-start
  0.6 1.0 %copy-done = bf16[2,256,512]{2,1,0:T(8,128)(2,1)S(1)} copy-done((bf16[2,256,512]{2,1,0:T(8,128)(2,1)S(1)}, bf16[2,256,512]{2,1,0:T(8,128)(2,1)}, u32[]{:S(2)}) %copy-start) | copy-done | bytes 524312
  1.7 0.9 copy-done.1
  2.6 38.6 %attention.1 = bf16[256,512]{1,0:T(8,128)(2,1)S(1)} custom-call(bf16[256,512]{1,0:T(8,128)(2,1)S(1)} %copy-done.1, bf16[2,256,512]{2,1,0:T(8,128)(2,1)S(1)} %copy-done), custom_call_target="tpu_custom_call" | custom-call | tf_op jit(solution)/shard_map/attention/pallas_call | solution.py:277
  41.3 0.1 copy.9
  41.4 1.5 %broadcast_in_dim.2 = bf16[8,256,512]{1,2,0:T(8,128)(2,1)} broadcast(bf16[256,512]{0,1:T(8,128)(2,1)S(1)} %copy.9), dimensions={1,2} | broadcast | bytes 2359296 | tf_op jit(solution)/shard_map/broadcast_in_dim | solution.py:328
  42.9 5.1 %all-to-all-start = ((bf16[8,256,512]{1,2,0:T(8,128)(2,1)}), bf16[8,256,512]{1,2,0:T(8,128)(2,1)S(1)}, u32[]{:S(2)}, u32[]{:S(2)}) async-start(bf16[8,256,512]{1,2,0:T(8,128)(2,1)} %broadcast_in_dim.2), calls=%async_computation | async-start | bytes 4194304 | tf_op jit(solution)/shard_map/all_to_all | solution.py:327
  48.0 0.7 fusion.32
  48.8 1.9 %collective-permute-start = (bf16[8,1024]{1,0:T(8,128)(2,1)S(1)}, bf16[8,1024]{1,0:T(8,128)(2,1)S(1)}, u32[]{:S(2)}, u32[]{:S(2)}) collective-permute-start(bf16[8,1024]{1,0:T(8,128)(2,1)S(1)} %get-tuple-element.28), channel_id=1, source_target_pairs={{0,8},{8,16},{16,24},{24,32},{32,40},{40,48},{48,56},{56,64},{64,7... | collective-permute-start | bytes 49160 | tf_op jit(solution)/shard_map/ppermute | solution.py:313
  50.7 7.3 %collective-permute-start.1 = (bf16[8,1024]{1,0:T(8,128)(2,1)S(1)}, bf16[8,1024]{1,0:T(8,128)(2,1)S(1)}, u32[]{:S(2)}, u32[]{:S(2)}) collective-permute-start(bf16[8,1024]{1,0:T(8,128)(2,1)S(1)} %get-tuple-element.29), channel_id=1, source_target_pairs={{8,0},{16,8},{24,16},{32,24},{40,32},{48,40},{56,48},{64,56},{72,6... | collective-permute-start | bytes 49160 | tf_op jit(solution)/shard_map/ppermute | solution.py:314
  58.0 0.0 copy-done.2
  58.0 0.0 copy-done.3
  58.0 20.3 %all-to-all-done = bf16[8,256,512]{1,2,0:T(8,128)(2,1)S(1)} async-done(((bf16[8,256,512]{1,2,0:T(8,128)(2,1)}), bf16[8,256,512]{1,2,0:T(8,128)(2,1)S(1)}, u32[]{:S(2)}, u32[]{:S(2)}) %all-to-all-start) | async-done | bytes 2097184 | tf_op jit(solution)/shard_map/all_to_all | solution.py:327
  78.3 6.6 %fusion.34 = (bf16[256,1024]{1,0:T(8,128)(2,1)}, f32[256,1024]{1,0:T(8,128)S(1)}) fusion(bf16[256,4096]{0,1:T(8,128)(2,1)S(1)} %bitcast.5, bf16[4096,1024]{1,0:T(8,128)(2,1)} %param.14, bf16[256,1024]{1,0:T(8,128)(2,1)} %param.11), kind=kOutput, calls=%fused_computation.27 | convolution fusion | flops 2148270080 | bytes 12582912 | tf_op jit(solution)/shard_map/dot_general | solution.py:356
  84.9 0.0 collective-permute-done
  84.9 0.0 collective-permute-done.1
  84.9 2.8 %fusion.35 = (bf16[400,1024]{1,0:T(8,128)(2,1)}, f32[400,1024]{1,0:T(8,128)S(1)}) fusion(f32[256,1024]{1,0:T(8,128)S(1)} %get-tuple-element.33, bf16[8,1024]{1,0:T(8,128)(2,1)S(1)} %collective-permute-done.1, bf16[384,1024]{1,0:T(8,128)(2,1)} %param.15, bf16[8,1024]{1,0:T(8,128)(2,1)S(1)} %collective-permute-done, f32[256]{0:T(256)S(1)} %get-tuple-element.31, ...), kind=kOutput, calls=%fused_computation.28 | convolution fusion | flops 423960576 | bytes 4330048 | tf_op jit(solution)/shard_map/dot_general | solution.py:360
  87.7 0.7 fusion.31
  88.5 1.9 %collective-permute-start.2 = (bf16[8,1024]{1,0:T(8,128)(2,1)S(1)}, bf16[8,1024]{1,0:T(8,128)(2,1)S(1)}, u32[]{:S(2)}, u32[]{:S(2)}) collective-permute-start(bf16[8,1024]{1,0:T(8,128)(2,1)S(1)} %get-tuple-element.27), channel_id=1, source_target_pairs={{8,0},{16,8},{24,16},{32,24},{40,32},{48,40},{56,48},{64,56},{72,6... | collective-permute-start | bytes 49160 | tf_op jit(solution)/shard_map/ppermute | solution.py:340
  90.4 2.4 %collective-permute-start.3 = (bf16[8,1024]{1,0:T(8,128)(2,1)S(1)}, bf16[8,1024]{1,0:T(8,128)(2,1)S(1)}, u32[]{:S(2)}, u32[]{:S(2)}) collective-permute-start(bf16[8,1024]{1,0:T(8,128)(2,1)S(1)} %get-tuple-element.26), channel_id=1, source_target_pairs={{0,8},{8,16},{16,24},{24,32},{32,40},{40,48},{48,56},{56,64},{64,7... | collective-permute-start | bytes 49160 | tf_op jit(solution)/shard_map/ppermute | solution.py:340
  92.8 0.2 slice.63
  93.0 0.0 collective-permute-done.2
  93.0 6.1 %collective-permute-done.3 = bf16[8,1024]{1,0:T(8,128)(2,1)S(1)} collective-permute-done((bf16[8,1024]{1,0:T(8,128)(2,1)S(1)}, bf16[8,1024]{1,0:T(8,128)(2,1)S(1)}, u32[]{:S(2)}, u32[]{:S(2)}) %collective-permute-start.3) | collective-permute-done | bytes 16416 | tf_op jit(solution)/shard_map/ppermute | solution.py:340
  99.1 1.0 convert_element_type.30
  (7 shorter events, 0.0 us)
Async XLA Ops:
  0.6 1.0 %copy-start = (bf16[2,256,512]{2,1,0:T(8,128)(2,1)S(1)}, bf16[2,256,512]{2,1,0:T(8,128)(2,1)}, u32[]{:S(2)}) copy-start(bf16[2,256,512]{2,1,0:T(8,128)(2,1)} %kv_ref.1) | copy-start | bytes 1572868
  1.7 0.9 copy-start.1
  42.9 15.1 %copy-start.2 = (s32[256]{0:T(256)S(1)}, s32[256]{0:T(256)}, u32[]{:S(2)}) copy-start(s32[256]{0:T(256)} %param.17) | copy-start | bytes 3076
  42.9 15.1 %copy-start.3 = (s32[256]{0:T(256)S(1)}, s32[256]{0:T(256)}, u32[]{:S(2)}) copy-start(s32[256]{0:T(256)} %param.16) | copy-start | bytes 3076
  42.9 35.4 %all-to-all-start = ((bf16[8,256,512]{1,2,0:T(8,128)(2,1)}), bf16[8,256,512]{1,2,0:T(8,128)(2,1)S(1)}, u32[]{:S(2)}, u32[]{:S(2)}) async-start(bf16[8,256,512]{1,2,0:T(8,128)(2,1)} %broadcast_in_dim.2), calls=%async_computation | async-start | bytes 4194304 | tf_op jit(solution)/shard_map/all_to_all | solution.py:327
  48.8 36.1 %collective-permute-start = (bf16[8,1024]{1,0:T(8,128)(2,1)S(1)}, bf16[8,1024]{1,0:T(8,128)(2,1)S(1)}, u32[]{:S(2)}, u32[]{:S(2)}) collective-permute-start(bf16[8,1024]{1,0:T(8,128)(2,1)S(1)} %get-tuple-element.28), channel_id=1, source_target_pairs={{0,8},{8,16},{16,24},{24,32},{32,40},{40,48},{48,56},{56,64},{64,7... | collective-permute-start | bytes 49160 | tf_op jit(solution)/shard_map/ppermute | solution.py:313
  50.7 34.2 %collective-permute-start.1 = (bf16[8,1024]{1,0:T(8,128)(2,1)S(1)}, bf16[8,1024]{1,0:T(8,128)(2,1)S(1)}, u32[]{:S(2)}, u32[]{:S(2)}) collective-permute-start(bf16[8,1024]{1,0:T(8,128)(2,1)S(1)} %get-tuple-element.29), channel_id=1, source_target_pairs={{8,0},{16,8},{24,16},{32,24},{40,32},{48,40},{56,48},{64,56},{72,6... | collective-permute-start | bytes 49160 | tf_op jit(solution)/shard_map/ppermute | solution.py:314
  88.5 4.5 %collective-permute-start.2 = (bf16[8,1024]{1,0:T(8,128)(2,1)S(1)}, bf16[8,1024]{1,0:T(8,128)(2,1)S(1)}, u32[]{:S(2)}, u32[]{:S(2)}) collective-permute-start(bf16[8,1024]{1,0:T(8,128)(2,1)S(1)} %get-tuple-element.27), channel_id=1, source_target_pairs={{8,0},{16,8},{24,16},{32,24},{40,32},{48,40},{56,48},{64,56},{72,6... | collective-permute-start | bytes 49160 | tf_op jit(solution)/shard_map/ppermute | solution.py:340
  90.4 8.7 %collective-permute-start.3 = (bf16[8,1024]{1,0:T(8,128)(2,1)S(1)}, bf16[8,1024]{1,0:T(8,128)(2,1)S(1)}, u32[]{:S(2)}, u32[]{:S(2)}) collective-permute-start(bf16[8,1024]{1,0:T(8,128)(2,1)S(1)} %get-tuple-element.26), channel_id=1, source_target_pairs={{0,8},{8,16},{16,24},{24,32},{32,40},{40,48},{48,56},{56,64},{64,7... | collective-permute-start | bytes 49160 | tf_op jit(solution)/shard_map/ppermute | solution.py:340

commit v2 on v1

--- a/solution.py
+++ b/solution.py
@@ -15,6 +15,14 @@
 MESH = pl.DeviceIdType.MESH
 EXP_SCALE = math.log2(math.e) / math.sqrt(HD)
 LOW = -1e30
+
+TEACH = 384
+EDGE = 16
+WINDOW = TEACH + 2 * EDGE
+DEPTH = 512
+WIDTH = 1024
+QUARTER = S_DEV // 4
+TILE = 256
 
 
 def pick(step, table):
@@ -297,77 +305,258 @@
             pltpu.SemaphoreType.DMA((2,)),
         ],
         compiler_params=pltpu.CompilerParams(
-            collective_id=0, has_side_effects=True, vmem_limit_bytes=40 << 20
+            collective_id=0, has_side_effects=True, vmem_limit_bytes=60 << 20
         ),
         name="attention",
     )(queries, keys_values)
 
 
-def with_halo(array, sides, width):
-    for axis, dim in sides:
-        peers, length = (lax.axis_size(axis), array.shape[dim])
-        up = [(i, (i + 1) % peers) for i in range(peers - 1)]
-        down = [(j, i) for i, j in up]
-        last = lax.slice_in_dim(array, length - width, length, axis=dim)
-        leading = lax.slice_in_dim(array, 0, width, axis=dim)
-        before = lax.ppermute(last, axis, up)
-        after = lax.ppermute(leading, axis, down)
-        array = jnp.concatenate([before, array, after], axis=dim)
-    return array
-
-
-def in_order(blocks, dim):
-    shape = list(blocks.shape[1:])
-    shape[dim] *= blocks.shape[0]
-    return jnp.moveaxis(blocks, 0, dim).reshape(shape)
-
-
-def sent_to_all(array, axis):
-    peers = lax.axis_size(axis)
-    return lax.all_to_all(
-        jnp.broadcast_to(array[None], (peers, *array.shape)), axis, 0, 0, tiled=True
+def project_kernel(
+    att_ref, student_ref, weight_ref, teacher_ref, start_ref, len_ref, out_ref, grad_ref,
+    att, weight, student, ext, member, member_t, accum, target, counts, edges, landed,
+    recv, send_right, send_left, send_pair, load, load_weight, edge_send, edge_recv,
+):
+    ctx, tp = lax.axis_index("ctx"), lax.axis_index("tp")
+    x, y_lo = tp // 2, tp % 2
+    pair = tp + 1 - 2 * y_lo
+    right, left = ((x + 1) % 4) * 2 + y_lo, ((x + 3) % 4) * 2 + y_lo
+    above, below = (ctx + 1) % 32, (ctx + 31) % 32
+
+    def slot_at(steps, same):
+        return ((x + steps + 4) % 4) * 2 + (y_lo if same else 1 - y_lo)
+
+    def piece(slot, q):
+        return att.at[slot, pl.ds(q * QUARTER, QUARTER)]
+
+    def copy(slot, q, to_tp, sems):
+        return pltpu.make_async_remote_copy(
+            src_ref=piece(slot, q), dst_ref=piece(slot, q), send_sem=sems.at[slot, q],
+            recv_sem=recv.at[slot, q], device_id=(ctx, to_tp), device_id_type=MESH,
+        )
+
+    to_right = lambda slot, q: copy(slot, q, right, send_right)
+    to_left = lambda slot, q: copy(slot, q, left, send_left)
+    to_pair = lambda slot, q: copy(slot, q, pair, send_pair)
+
+    def arrived(slot, q):
+        to_pair(slot, q).wait_recv()
+
+    def edge_copy(k):
+        to_ctx = above if k == 0 else below
+        src = teacher_ref.at[pl.ds(TEACH - EDGE, EDGE)] if k == 0 else teacher_ref.at[pl.ds(0, EDGE)]
+        dst = ext.at[pl.ds(0, EDGE)] if k == 0 else ext.at[pl.ds(EDGE + TEACH, EDGE)]
+        return pltpu.make_async_remote_copy(
+            src_ref=src, dst_ref=dst, send_sem=edge_send.at[k], recv_sem=edge_recv.at[k],
+            device_id=(to_ctx, tp), device_id_type=MESH,
+        )
+
+    def grad_copy(k):
+        return pltpu.make_async_remote_copy(
+            src_ref=edges.at[k], dst_ref=landed.at[k], send_sem=edge_send.at[2 + k],
+            recv_sem=edge_recv.at[2 + k], device_id=(above if k == 0 else below, tp),
+            device_id_type=MESH,
+        )
+
+    def weight_load(slot):
+        rows = pl.ds(pl.multiple_of(slot * DEPTH, DEPTH), DEPTH)
+        return pltpu.make_async_copy(weight_ref.at[rows], weight.at[rows], load_weight.at[slot])
+
+    own_load = pltpu.make_async_copy(att_ref, att.at[tp], load.at[0])
+    student_load = pltpu.make_async_copy(student_ref, student, load.at[1])
+    teacher_load = pltpu.make_async_copy(teacher_ref, ext.at[pl.ds(EDGE, TEACH)], load.at[2])
+    own_load.start()
+    barrier = pltpu.get_barrier_semaphore()
+    for to_ctx, to_tp in ((ctx, right), (ctx, left), (ctx, pair), (above, tp), (below, tp)):
+        pl.semaphore_signal(barrier, inc=1, device_id=(to_ctx, to_tp), device_id_type=MESH)
+    own_load.wait()
+    pl.semaphore_wait(barrier, 5)
+
+    for k in range(4):
+        to_pair(tp, (2, 3, 0, 1)[k]).start()
+        to_right(tp, (0, 2, 1, 3)[k]).start()
+        to_left(tp, (1, 3, 0, 2)[k]).start()
+    for k in range(2):
+        edge_copy(k).start()
+    student_load.start()
+    teacher_load.start()
+    order = [
+        tp, pair, slot_at(-1, True), slot_at(1, True), slot_at(2, True),
+        slot_at(-1, False), slot_at(1, False), slot_at(2, False),
+    ]
+    for slot in order:
+        weight_load(slot).start()
+
+    ext[WINDOW:, :] = jnp.zeros((ext.shape[0] - WINDOW, WIDTH), jnp.bfloat16)
+    first = ctx * TEACH - EDGE
+    start_row, len_row = start_ref[...], len_ref[...]
+    row_pos = first + lax.broadcasted_iota(jnp.int32, (WINDOW, S_DEV), 0)
+    inside = (row_pos >= start_row) & (row_pos < start_row + len_row)
+    member_t[...] = jnp.where(inside, 1.0, 0.0).astype(jnp.bfloat16)
+    wide_start = jnp.broadcast_to(start_row.astype(jnp.float32), (HD, S_DEV)).T[:, :1]
+    wide_len = jnp.broadcast_to(len_row.astype(jnp.float32), (HD, S_DEV)).T
+    counts[...] = 1.0 / wide_len
+    col_pos = (first + lax.broadcasted_iota(jnp.int32, member.shape, 1)).astype(jnp.float32)
+    inside = (col_pos >= wide_start) & (col_pos < wide_start + wide_len[:, :1])
+    member[...] = jnp.where(inside, 1.0, 0.0).astype(jnp.bfloat16)
+    student_load.wait()
+    accum[...] = student[...].astype(jnp.float32)
+
+    def columns(j):
+        return pl.ds(pl.multiple_of(j * TILE, TILE), TILE)
+
+    def multiply(slot):
+        weight_load(slot).wait()
+        rows = pl.ds(pl.multiple_of(slot * DEPTH, DEPTH), DEPTH)
+
+        @pl.loop(0, WIDTH // TILE)
+        def _(j):
+            accum[:, columns(j)] += jnp.dot(
+                att[slot], weight[rows, columns(j)], preferred_element_type=jnp.float32
+            )
+
+    prev, nxt = slot_at(-1, True), slot_at(1, True)
+    far, far_other = slot_at(2, True), slot_at(2, False)
+    prev_other, nxt_other = slot_at(-1, False), slot_at(1, False)
+
+    arrived(pair, 2)
+    to_right(pair, 2).start()
+    to_left(pair, 2).start()
+    arrived(pair, 3)
+    to_left(pair, 3).start()
+    to_right(pair, 3).start()
+    multiply(tp)
+    arrived(prev, 0)
+    to_right(prev, 0).start()
+    to_pair(prev, 0).start()
+    arrived(nxt, 1)
+    to_left(nxt, 1).start()
+    to_pair(nxt, 1).start()
+    arrived(prev, 2)
+    to_right(prev, 2).start()
+    arrived(nxt, 3)
+    to_left(nxt, 3).start()
+    arrived(prev, 1)
+    to_pair(prev, 1).start()
+    arrived(nxt, 0)
+    to_pair(nxt, 0).start()
+    teacher_load.wait()
+    for k in range(2):
+        edge_copy(k).wait_recv()
+
+    @pl.loop(0, WIDTH // TILE)
+    def _(j):
+        summed = jnp.dot(member[...], ext[:, columns(j)], preferred_element_type=jnp.float32)
+        target[:, columns(j)] = summed * counts[:, :1]
+
+    arrived(pair, 0)
+    arrived(pair, 1)
+    arrived(prev_other, 2)
+    to_right(prev_other, 2).start()
+    arrived(nxt_other, 3)
+    to_left(nxt_other, 3).start()
+    multiply(pair)
+    arrived(far, 0)
+    to_pair(far, 0).start()
+    arrived(far, 1)
+    to_pair(far, 1).start()
+    arrived(prev, 3)
+    multiply(prev)
+    arrived(nxt, 2)
+    multiply(nxt)
+    for q in (2, 3):
+        arrived(far, q)
+    multiply(far)
+    for q in (3, 0, 1):
+        arrived(prev_other, q)
+    multiply(prev_other)
+    for q in (2, 0, 1):
+        arrived(nxt_other, q)
+    multiply(nxt_other)
+    for q in (2, 3, 0, 1):
+        arrived(far_other, q)
+    weight_load(far_other).wait()
+    last_rows = pl.ds(pl.multiple_of(far_other * DEPTH, DEPTH), DEPTH)
+
+    @pl.loop(0, WIDTH // TILE)
+    def _(j):
+        student32 = accum[:, columns(j)] + jnp.dot(
+            att[far_other], weight[last_rows, columns(j)], preferred_element_type=jnp.float32
+        )
+        out_ref[:, columns(j)] = student32.astype(jnp.bfloat16)
+        weighted = ((student32 - target[:, columns(j)]) * counts[:, :1]).astype(jnp.bfloat16)
+        spread = jnp.dot(member_t[...], weighted, preferred_element_type=jnp.float32)
+        edges[0, :, columns(j)] = spread[EDGE + TEACH : EDGE + TEACH + HALO]
+        edges[1, :, columns(j)] = spread[EDGE - HALO : EDGE]
+        accum[:, columns(j)] = spread[EDGE : EDGE + S_DEV]
+        target[: TEACH - S_DEV, columns(j)] = spread[EDGE + S_DEV : EDGE + TEACH]
+
+    for k in range(2):
+        grad_copy(k).start()
+    grad_ref[EDGE:S_DEV, :] = accum[EDGE:, :].astype(jnp.bfloat16)
+    rest = TEACH - S_DEV - EDGE
+    grad_ref[S_DEV : TEACH - EDGE, :] = target[:rest, :].astype(jnp.bfloat16)
+    for k in range(2):
+        grad_copy(k).wait_recv()
+    low = accum[:EDGE, :] + jnp.concatenate([landed[0], jnp.zeros_like(landed[0])], axis=0)
+    grad_ref[:EDGE, :] = low.astype(jnp.bfloat16)
+    high = target[rest : rest + EDGE, :] + jnp.concatenate(
+        [jnp.zeros_like(landed[1]), landed[1]], axis=0
     )
-
-
-def collect(array, axis, dim):
-    blocks = sent_to_all(array, axis)
-    return in_order(blocks, dim)
-
-
-def shifted(value, axis, steps):
-    count = lax.axis_size(axis)
-    leading, last = (max(0, -steps), min(count, count - steps))
-    return lax.ppermute(value, axis, [(source, source + steps) for source in range(leading, last)])
+    grad_ref[TEACH - EDGE :, :] = high.astype(jnp.bfloat16)
+
+    for k in range(2):
+        edge_copy(k).wait_send()
+        grad_copy(k).wait_send()
+    for q in range(4):
+        to_pair(tp, q).wait_send()
+        to_right(tp, q).wait_send()
+        to_left(tp, q).wait_send()
+    for q in (2, 3):
+        to_right(pair, q).wait_send()
+        to_left(pair, q).wait_send()
+    for slot, q in ((prev, 0), (prev, 2), (prev_other, 2)):
+        to_right(slot, q).wait_send()
+    for slot, q in ((nxt, 1), (nxt, 3), (nxt_other, 3)):
+        to_left(slot, q).wait_send()
+    for slot in (prev, nxt, far):
+        for q in range(2):
+            to_pair(slot, q).wait_send()
 
 
 def body(student_rows, queries, keys_values, out_weight, teacher_rows, span_start, span_len):
-    ctx_rank = lax.axis_index("ctx")
-    teach_dev = teacher_rows.shape[0]
-    extended = with_halo(teacher_rows, (("ctx", 0),), HALO)
-    window = teach_dev + 2 * HALO
-    columns = ctx_rank * teach_dev - HALO + jnp.arange(window)
-    span_end = span_start + span_len
-    member = (
-        (columns[None, :] >= span_start[:, None]) & (columns[None, :] < span_end[:, None])
-    ).astype(jnp.bfloat16)
-    span_counts = span_len.astype(jnp.float32)[:, None]
-    target = jnp.dot(member, extended, preferred_element_type=jnp.float32) / span_counts
     attended = attention(queries, keys_values)
-    projected = jnp.dot(collect(attended, "tp", 1), out_weight, preferred_element_type=jnp.float32)
-    student32 = student_rows.astype(jnp.float32) + projected
-    resid = student32 - target
-    weighted = (resid / span_counts).astype(jnp.bfloat16)
-    spread = lax.dot_general(
-        member, weighted, (((0,), (0,)), ((), ())), preferred_element_type=jnp.float32
+    in_vmem, anywhere = pl.BlockSpec(memory_space=pltpu.VMEM), pl.BlockSpec(memory_space=pl.ANY)
+    dma = pltpu.SemaphoreType.DMA
+    return pl.pallas_call(
+        project_kernel,
+        out_shape=(
+            jax.ShapeDtypeStruct((S_DEV, WIDTH), jnp.bfloat16),
+            jax.ShapeDtypeStruct((TEACH, WIDTH), jnp.bfloat16),
+        ),
+        in_specs=[anywhere, anywhere, anywhere, anywhere, in_vmem, in_vmem],
+        out_specs=(in_vmem, in_vmem),
+        scratch_shapes=[
+            pltpu.VMEM((8, S_DEV, DEPTH), jnp.bfloat16),
+            pltpu.VMEM((8 * DEPTH, WIDTH), jnp.bfloat16),
+            pltpu.VMEM((S_DEV, WIDTH), jnp.bfloat16),
+            pltpu.VMEM((512, WIDTH), jnp.bfloat16),
+            pltpu.VMEM((S_DEV, 512), jnp.bfloat16),
+            pltpu.VMEM((WINDOW, S_DEV), jnp.bfloat16),
+            pltpu.VMEM((S_DEV, WIDTH), jnp.float32),
+            pltpu.VMEM((S_DEV, WIDTH), jnp.float32),
+            pltpu.VMEM((S_DEV, HD), jnp.float32),
+            pltpu.VMEM((2, HALO, WIDTH), jnp.float32),
+            pltpu.VMEM((2, HALO, WIDTH), jnp.float32),
+            dma((8, 4)), dma((8, 4)), dma((8, 4)), dma((8, 4)), dma((3,)), dma((8,)), dma((4,)), dma((4,)),
+        ],
+        compiler_params=pltpu.CompilerParams(
+            collective_id=1, has_side_effects=True, vmem_limit_bytes=60 << 20
+        ),
+        name="project",
+    )(
+        attended, student_rows, out_weight, teacher_rows,
+        span_start.reshape(1, S_DEV), span_len.reshape(1, S_DEV),
     )
-    from_above = shifted(spread[:HALO].astype(jnp.bfloat16), "ctx", -1).astype(jnp.float32)
-    from_below = shifted(spread[teach_dev + HALO :].astype(jnp.bfloat16), "ctx", 1).astype(
-        jnp.float32
-    )
-    core = spread[HALO : HALO + teach_dev]
-    core = core.at[teach_dev - HALO :].add(from_above)
-    core = core.at[:HALO].add(from_below)
-    return (student32.astype(jnp.bfloat16), core.astype(jnp.bfloat16))
 
 
 def solution(mesh):

time: 101 us -> 75.9 us (0.75)
  the two profiles are of different devices: /device:TPU:16 before, /device:TPU:2 now
where the time goes in v2:
time: 75.9 us; the launch traced here: 75.6 us
  Pallas kernels  71 us (94%)
  local copies, waits for them, and re-layouts  3.93 us (5%)
    pallas_call x1, Pallas kernels, body(): pl.pallas_call(project_kernel, out_shape=(jax.ShapeDtypeStruct((S_DEV, WI...  43.4 us
    pallas_call x1, Pallas kernels, attention(): pl.pallas_call(attend_kernel, out_shape=jax.ShapeDtypeStruct(queries.shap...  27.7 us
    unnamed x2, local copies, waits for them, and re-layouts  3.93 us

profile of v2, /device:TPU:2, one launch (start us, length us, event | category | flops | bytes accessed | tf_op | source)
XLA Modules:
  0.0 75.6 jit_solution(11321834165740177281)
XLA Ops:
  0.6 27.7 %attention.1.att_ref = bf16[256,512]{1,0:T(8,128)(2,1)} custom-call(bf16[256,512]{1,0:T(8,128)(2,1)} %q_ref.1, bf16[2,256,512]{2,1,0:T(8,128)(2,1)} %kv_ref.1), custom_call_target="tpu_custom_call" | custom-call | tf_op jit(solution)/shard_map/attention/pallas_call | solution.py:285
  28.3 43.4 %project.1 = (bf16[256,1024]{1,0:T(8,128)(2,1)}, bf16[384,1024]{1,0:T(8,128)(2,1)}) custom-call(bf16[256,512]{1,0:T(8,128)(2,1)} %attention.1.att_ref, bf16[256,1024]{1,0:T(8,128)(2,1)} %student_ref.1, bf16[4096,1024]{1,0:T(8,128)(2,1)} %weight_ref.1, bf16[384,1024]{1,0:T(8,128)(2,1)} %teacher_ref.1, s32[1,256]{1,0:T(1,128)} %bitcast.2, s32[1,256]{1,0:T(1,128)} %bitcast.3), custom_call_target="tpu_custom_call" | custom-call | tf_op jit(solution)/shard_map/project/pallas_call | solution.py:530
  71.7 1.9 %copy.11 = bf16[256,1024]{1,0:T(8,128)(2,1)} copy(bf16[256,1024]{1,0:T(8,128)(2,1)} %get-tuple-element.4) | data formatting | bytes 1048576
  73.5 2.1 %copy.12 = bf16[384,1024]{1,0:T(8,128)(2,1)} copy(bf16[384,1024]{1,0:T(8,128)(2,1)} %get-tuple-element.5) | data formatting | bytes 1572864

commit v3 on v1

v3 whole, which is shorter than its diff:
```python
import functools
import math

import jax
import jax.numpy as jnp
from jax import lax
from jax.experimental import pallas as pl
from jax.experimental.pallas import tpu as pltpu
from jax.sharding import PartitionSpec as P

HD = 128
S_DEV = 256
HALO = 8
N_Z = 8
MESH = pl.DeviceIdType.MESH
EXP_SCALE = math.log2(math.e) / math.sqrt(HD)
LOW = -1e30

TEACH = 384
EDGE = 16
WINDOW = TEACH + 2 * EDGE
DEPTH = 512
WIDTH = 1024
QUARTER = S_DEV // 4
TILE = 256


def pick(step, table):
    value = table[0]
    for k in range(1, len(table)):
        value = jnp.where(step == k, table[k], value)
    return value


def layer_kernel(
    q_ref, kv_ref, student_ref, weight_ref, teacher_ref, start_ref, len_ref, out_ref, grad_ref,
    buf, own_v, q_rows, q_t, scores, peak, decay, total, accum,
    att, weight, student, ext, member, member_t, result, target, counts, edges, landed,
    recv, recv_sib, send_right, send_left, send_sib, send_cross, send_pair,
    x_recv, x_send_right, x_send_left, x_send_pair, load, load_weight, edge_send, edge_recv,
):
    ctx, tp = lax.axis_index("ctx"), lax.axis_index("tp")
    core, z, y_hi = ctx % 2, (ctx // 2) % N_Z, ctx // 16
    x, y_lo = tp // 2, tp % 2
    sibling = ctx + 1 - 2 * core
    right = y_hi * 16 + ((z + 1) % N_Z) * 2 + core
    left = y_hi * 16 + ((z + N_Z - 1) % N_Z) * 2 + core
    other_hi = (ctx + 16) % 32
    pair = tp + 1 - 2 * y_lo
    kind_on = jnp.where(y_hi == 0, y_lo, 1 - y_lo)
    kind_swap = 1 - kind_on
    x_right, x_left = ((x + 1) % 4) * 2 + y_lo, ((x + 3) % 4) * 2 + y_lo
    above, below = (ctx + 1) % 32, (ctx + 31) % 32

    def at(hi, steps):
        return hi * 16 + ((z + steps + N_Z) % N_Z) * 2 + core

    def piece(kind, slot, p):
        return buf.at[kind, pl.ds(pl.multiple_of(slot * S_DEV + p * HD, HD), HD)]

    def part(kind, slot):
        return buf.at[kind, pl.ds(pl.multiple_of(slot * S_DEV, S_DEV), S_DEV)]

    def copy(kind, slot, p, to_ctx, to_tp, sem):
        return pltpu.make_async_remote_copy(
            src_ref=piece(kind, slot, p), dst_ref=piece(kind, slot, p), send_sem=sem,
            recv_sem=recv.at[kind, slot * 2 + p], device_id=(to_ctx, to_tp), device_id_type=MESH,
        )

    def arrived(kind, slot, p):
        copy(kind, slot, p, ctx, pair, send_pair.at[0]).wait_recv()

    def to_sibling(kind, slot):
        return pltpu.make_async_remote_copy(
            src_ref=part(kind, slot), dst_ref=part(kind, slot), send_sem=send_sib.at[kind, slot],
            recv_sem=recv_sib.at[kind, slot], device_id=(sibling, tp), device_id_type=MESH,
        )

    def to_right(kind, hops, p):
        return copy(kind, at(y_hi, -hops), p, right, tp, send_right.at[kind, hops * 2 + p])

    def to_left(kind, hops, p):
        return copy(kind, at(y_hi, hops), p, left, tp, send_left.at[kind, hops * 2 + p])

    def to_cross(slot, p):
        return copy(y_lo, slot, p, other_hi, pair, send_cross.at[slot // 2 % N_Z * 2 + p])

    def to_pair(slot, p):
        return copy(kind_on, slot, p, ctx, pair, send_pair.at[slot // 2 % N_Z * 2 + p])

    k_load = pltpu.make_async_copy(
        kv_ref.at[0, :, pl.ds(pl.multiple_of(x * HD, HD), HD)], part(0, ctx), load.at[3]
    )
    v_load = pltpu.make_async_copy(
        kv_ref.at[1, :, pl.ds(pl.multiple_of(x * HD, HD), HD)], own_v, load.at[0]
    )
    q_load = pltpu.make_async_copy(q_ref, q_rows, load.at[4])
    v_load.start()
    k_load.start()
    q_load.start()
    barrier = pltpu.get_barrier_semaphore()
    for to_ctx, to_tp in (
        (right, tp), (left, tp), (sibling, tp), (other_hi, pair), (ctx, pair),
        (ctx, x_right), (ctx, x_left), (above, tp), (below, tp),
    ):
        pl.semaphore_signal(barrier, inc=1, device_id=(to_ctx, to_tp), device_id_type=MESH)
    v_load.wait()
    v_own = own_v[...].astype(jnp.float32)
    for half in range(2):
        turned = v_own[half * HD : (half + 1) * HD].T.astype(jnp.bfloat16)
        start = pl.multiple_of(ctx * S_DEV + half * HD, HD)
        buf[1, pl.ds(start, HD), :] = turned
    q_load.wait()
    for h in range(4):
        q_t[:, h * S_DEV : (h + 1) * S_DEV] = (
            q_rows[:, h * HD : (h + 1) * HD].astype(jnp.float32).T.astype(jnp.bfloat16)
        )
    k_load.wait()
    pl.semaphore_wait(barrier, 9)

    def for_ring(action):
        @pl.when(y_hi == 0)
        def _():
            action([y_lo])

        @pl.when(y_hi == 1)
        def _():
            action([0, 1])

    def start_own(kinds):
        for p in range(2):
            for kind in kinds:
                to_right(kind, 0, p).start()
                to_left(kind, 0, 1 - p).start()
            if len(kinds) == 1:
                to_cross(ctx, p).start()

    for_ring(start_own)
    for kind in range(2):
        to_sibling(kind, ctx).start()

    def ring(hops, kinds):
        def side(kind, moving_right, p):
            slot = at(y_hi, -hops if moving_right else hops)
            arrived(kind, slot, p)
            last = 3 if (p == 0) == moving_right else 2
            if hops <= last:
                (to_right if moving_right else to_left)(kind, hops, p).start()
            if len(kinds) == 1:
                to_cross(slot, p).start()
                to_pair(slot, p).start()

        if hops < 4:
            for k in range(2):
                for kind in kinds:
                    side(kind, True, k)
                    side(kind, False, 1 - k)
            for kind in kinds:
                to_sibling(kind, at(y_hi, -hops)).start()
                to_sibling(kind, at(y_hi, hops)).start()
        else:
            for kind in kinds:
                side(kind, True, 0)
                side(kind, False, 1)
                to_sibling(kind, at(y_hi, 4)).start()

    def low_slots(hops):
        if hops in (0, 4):
            return [at(0, hops)]
        return [at(0, -hops), at(0, hops)]

    def from_cross(hops):
        for p in (0, 1):
            for k, slot in enumerate(low_slots(hops)):
                q = p if k == 0 else 1 - p
                arrived(kind_on, slot, q)
                to_pair(slot, q).start()
        for slot in low_slots(hops):
            to_sibling(kind_on, slot).start()

    def from_pair(hops):
        for slot in low_slots(hops):
            arrived(kind_swap, slot, 0)
            arrived(kind_swap, slot, 1)
            to_sibling(kind_swap, slot).start()


    def slot_at(steps, same):
        return ((x + steps + 4) % 4) * 2 + (y_lo if same else 1 - y_lo)

    def quarter(slot, q):
        return att.at[slot, pl.ds(q * QUARTER, QUARTER)]

    def send(slot, q, to_tp, sems):
        return pltpu.make_async_remote_copy(
            src_ref=quarter(slot, q), dst_ref=quarter(slot, q), send_sem=sems.at[slot, q],
            recv_sem=x_recv.at[slot, q], device_id=(ctx, to_tp), device_id_type=MESH,
        )

    x_to_right = lambda slot, q: send(slot, q, x_right, x_send_right)
    x_to_left = lambda slot, q: send(slot, q, x_left, x_send_left)
    x_to_pair = lambda slot, q: send(slot, q, pair, x_send_pair)

    def landed_at(slot, q):
        x_to_pair(slot, q).wait_recv()

    def edge_copy(k):
        to_ctx = above if k == 0 else below
        src = teacher_ref.at[pl.ds(TEACH - EDGE, EDGE)] if k == 0 else teacher_ref.at[pl.ds(0, EDGE)]
        dst = ext.at[pl.ds(0, EDGE)] if k == 0 else ext.at[pl.ds(EDGE + TEACH, EDGE)]
        return pltpu.make_async_remote_copy(
            src_ref=src, dst_ref=dst, send_sem=edge_send.at[k], recv_sem=edge_recv.at[k],
            device_id=(to_ctx, tp), device_id_type=MESH,
        )

    def grad_copy(k):
        return pltpu.make_async_remote_copy(
            src_ref=edges.at[k], dst_ref=landed.at[k], send_sem=edge_send.at[2 + k],
            recv_sem=edge_recv.at[2 + k], device_id=(above if k == 0 else below, tp),
            device_id_type=MESH,
        )

    def weight_load(slot):
        rows = pl.ds(pl.multiple_of(slot * DEPTH, DEPTH), DEPTH)
        return pltpu.make_async_copy(weight_ref.at[rows], weight.at[rows], load_weight.at[slot])

    student_load = pltpu.make_async_copy(student_ref, student, load.at[1])
    teacher_load = pltpu.make_async_copy(teacher_ref, ext.at[pl.ds(EDGE, TEACH)], load.at[2])
    def edge_and_loads():
        for k in range(2):
            edge_copy(k).start()
        student_load.start()
        teacher_load.start()
        order = [
            tp, pair, slot_at(-1, True), slot_at(1, True), slot_at(2, True),
            slot_at(-1, False), slot_at(1, False), slot_at(2, False),
        ]
        for slot in order:
            weight_load(slot).start()

    half_rows = 2 * S_DEV

    def score(block, c, masked=False):
        cols = slice(c * half_rows, (c + 1) * half_rows)
        keys = buf[0, pl.ds(pl.multiple_of(block * 2 * S_DEV, 2 * S_DEV), 2 * S_DEV), :]
        s = jnp.dot(keys, q_t[:, cols], preferred_element_type=jnp.float32)
        if masked:
            key_pos = lax.broadcasted_iota(jnp.int32, s.shape, 0)
            query_pos = lax.broadcasted_iota(jnp.int32, s.shape, 1) % S_DEV + core * S_DEV
            s = jnp.where(key_pos <= query_pos, s, LOW)
        scores[c] = s
        new_peak = jnp.max(s, axis=0, keepdims=True)
        if not masked:
            old = peak[:, cols]
            new_peak = jnp.maximum(old, new_peak)
            decay[:, cols] = jnp.exp2((old - new_peak) * EXP_SCALE)
        peak[:, cols] = new_peak

    def gather_values(block, c, first=False):
        cols = slice(c * half_rows, (c + 1) * half_rows)
        weights = jnp.exp2((scores[c] - peak[:, cols]) * EXP_SCALE)
        added = jnp.sum(weights, axis=0, keepdims=True)
        rounded = weights.astype(jnp.bfloat16)
        base = block * 2 * S_DEV
        product = None
        for k in range(2):
            parts = [
                buf[1, pl.ds(pl.multiple_of(base + k * S_DEV + g * HD, HD), HD), :]
                for g in range(2)
            ]
            values = jnp.concatenate(parts, axis=1)
            term = jnp.dot(
                values, rounded[k * S_DEV : (k + 1) * S_DEV], preferred_element_type=jnp.float32
            )
            product = term if product is None else product + term
        if first:
            total[:, cols] = added
            accum[:, cols] = product
        else:
            shrink = decay[:, cols]
            total[:, cols] = total[:, cols] * shrink + added
            accum[:, cols] = accum[:, cols] * shrink + product

    own_block = ctx // 2
    edge_and_loads()
    for kind in range(2):
        to_sibling(kind, sibling).wait_recv()
    score(own_block, 0, masked=True)
    score(own_block, 1, masked=True)
    gather_values(own_block, 0, first=True)
    total[:, half_rows:] = jnp.zeros((1, half_rows), jnp.float32)
    accum[:, half_rows:] = jnp.zeros((HD, half_rows), jnp.float32)
    decay[:, half_rows:] = jnp.ones((1, half_rows), jnp.float32)

    low_order = {2: (1, -1), 3: (1, 1), 4: (1, -2), 5: (1, 2), 7: (1, -3), 8: (1, 3), 9: (1, 4)}
    low_events = {
        1: [(ring, 1)], 2: [(from_pair, 1)], 3: [(ring, 2)], 4: [(from_pair, 2)], 5: [(ring, 3)],
        6: [(ring, 4)], 7: [(from_pair, 3)], 8: [(from_pair, 4)],
    }
    high_order = {
        1: (1, -1), 2: (1, 1), 3: (2, 0), 4: (1, -2), 5: (1, 2), 6: (2, -1), 7: (2, 1), 8: (1, -3),
        9: (1, 3), 10: (1, 4), 11: (2, -2), 12: (2, 2), 13: (2, -3), 14: (2, 3), 15: (2, 4),
    }
    high_events = {
        1: [(ring, 1), (from_cross, 0)], 2: [(ring, 2), (from_cross, 1), (from_pair, 0)],
        4: [(from_pair, 1)], 5: [(ring, 3), (from_cross, 2)], 7: [(from_pair, 2)],
        8: [(ring, 4), (from_cross, 3)], 10: [(from_pair, 3), (from_cross, 4)], 12: [(from_pair, 4)],
    }

    def lookup(n, field):
        low = pick(n, [low_order.get(k, (0, 0))[field] for k in range(16)])
        high = pick(n, [high_order.get(k, (0, 0))[field] for k in range(16)])
        return jnp.where(y_hi == 0, low, high)

    def step(n, before):
        plane = lookup(n, 0)
        block_z = (z + lookup(n, 1) + N_Z) % N_Z
        for hi, events, kinds in ((0, low_events, [y_lo]), (1, high_events, [0, 1])):
            @pl.when(y_hi == hi)
            def _(events=events, kinds=kinds):
                for k, todo in events.items():
                    @pl.when(n == k)
                    def _(todo=todo):
                        for action, hops in todo:
                            if action is ring:
                                ring(hops, kinds)
                            else:
                                action(hops)

        block = jnp.where(plane == 2, block_z, y_hi * N_Z + block_z)
        here = plane > 0

        @pl.when(here)
        def _():
            for kind in range(2):
                to_sibling(kind, block * 2 + 1 - core).wait_recv()

        def compute(prior):
            score(block, 0)
            gather_values(prior, 1)
            score(block, 1)
            gather_values(block, 0)
            return block

        return lax.cond(here & (block < own_block), compute, lambda prior: prior, before)

    last_block = lax.fori_loop(1, 16, step, own_block)
    gather_values(last_block, 1)
    for h in range(4):
        cols = slice(h * S_DEV, (h + 1) * S_DEV)
        att[tp, :, h * HD : (h + 1) * HD] = (accum[:, cols] / total[:, cols]).T.astype(jnp.bfloat16)


    for k in range(4):
        x_to_pair(tp, (2, 3, 0, 1)[k]).start()
        x_to_right(tp, (0, 2, 1, 3)[k]).start()
        x_to_left(tp, (1, 3, 0, 2)[k]).start()
    ext[WINDOW:, :] = jnp.zeros((ext.shape[0] - WINDOW, WIDTH), jnp.bfloat16)
    first = ctx * TEACH - EDGE
    start_row, len_row = start_ref[...], len_ref[...]
    row_pos = first + lax.broadcasted_iota(jnp.int32, (WINDOW, S_DEV), 0)
    inside = (row_pos >= start_row) & (row_pos < start_row + len_row)
    member_t[...] = jnp.where(inside, 1.0, 0.0).astype(jnp.bfloat16)
    wide_start = jnp.broadcast_to(start_row.astype(jnp.float32), (HD, S_DEV)).T[:, :1]
    wide_len = jnp.broadcast_to(len_row.astype(jnp.float32), (HD, S_DEV)).T
    counts[...] = 1.0 / wide_len
    col_pos = (first + lax.broadcasted_iota(jnp.int32, member.shape, 1)).astype(jnp.float32)
    inside = (col_pos >= wide_start) & (col_pos < wide_start + wide_len[:, :1])
    member[...] = jnp.where(inside, 1.0, 0.0).astype(jnp.bfloat16)
    student_load.wait()
    result[...] = student[...].astype(jnp.float32)

    def columns(j):
        return pl.ds(pl.multiple_of(j * TILE, TILE), TILE)

    def multiply(slot):
        weight_load(slot).wait()
        rows = pl.ds(pl.multiple_of(slot * DEPTH, DEPTH), DEPTH)

        @pl.loop(0, WIDTH // TILE)
        def _(j):
            result[:, columns(j)] += jnp.dot(
                att[slot], weight[rows, columns(j)], preferred_element_type=jnp.float32
            )

    prev, nxt = slot_at(-1, True), slot_at(1, True)
    far, far_other = slot_at(2, True), slot_at(2, False)
    prev_other, nxt_other = slot_at(-1, False), slot_at(1, False)

    landed_at(pair, 2)
    x_to_right(pair, 2).start()
    x_to_left(pair, 2).start()
    landed_at(pair, 3)
    x_to_left(pair, 3).start()
    x_to_right(pair, 3).start()
    multiply(tp)
    landed_at(prev, 0)
    x_to_right(prev, 0).start()
    x_to_pair(prev, 0).start()
    landed_at(nxt, 1)
    x_to_left(nxt, 1).start()
    x_to_pair(nxt, 1).start()
    landed_at(prev, 2)
    x_to_right(prev, 2).start()
    landed_at(nxt, 3)
    x_to_left(nxt, 3).start()
    landed_at(prev, 1)
    x_to_pair(prev, 1).start()
    landed_at(nxt, 0)
    x_to_pair(nxt, 0).start()
    teacher_load.wait()
    for k in range(2):
        edge_copy(k).wait_recv()

    @pl.loop(0, WIDTH // TILE)
    def _(j):
        summed = jnp.dot(member[...], ext[:, columns(j)], preferred_element_type=jnp.float32)
        target[:, columns(j)] = summed * counts[:, :1]

    landed_at(pair, 0)
    landed_at(pair, 1)
    landed_at(prev_other, 2)
    x_to_right(prev_other, 2).start()
    landed_at(nxt_other, 3)
    x_to_left(nxt_other, 3).start()
    multiply(pair)
    landed_at(far, 0)
    x_to_pair(far, 0).start()
    landed_at(far, 1)
    x_to_pair(far, 1).start()
    landed_at(prev, 3)
    multiply(prev)
    landed_at(nxt, 2)
    multiply(nxt)
    for q in (2, 3):
        landed_at(far, q)
    multiply(far)
    for q in (3, 0, 1):
        landed_at(prev_other, q)
    multiply(prev_other)
    for q in (2, 0, 1):
        landed_at(nxt_other, q)
    multiply(nxt_other)
    for q in (2, 3, 0, 1):
        landed_at(far_other, q)
    weight_load(far_other).wait()
    last_rows = pl.ds(pl.multiple_of(far_other * DEPTH, DEPTH), DEPTH)

    @pl.loop(0, WIDTH // TILE)
    def _(j):
        student32 = result[:, columns(j)] + jnp.dot(
            att[far_other], weight[last_rows, columns(j)], preferred_element_type=jnp.float32
        )
        out_ref[:, columns(j)] = student32.astype(jnp.bfloat16)
        weighted = ((student32 - target[:, columns(j)]) * counts[:, :1]).astype(jnp.bfloat16)
        spread = jnp.dot(member_t[...], weighted, preferred_element_type=jnp.float32)
        edges[0, :, columns(j)] = spread[EDGE + TEACH : EDGE + TEACH + HALO]
        edges[1, :, columns(j)] = spread[EDGE - HALO : EDGE]
        result[:, columns(j)] = spread[EDGE : EDGE + S_DEV]
        target[: TEACH - S_DEV, columns(j)] = spread[EDGE + S_DEV : EDGE + TEACH]

    for k in range(2):
        grad_copy(k).start()
    grad_ref[EDGE:S_DEV, :] = result[EDGE:, :].astype(jnp.bfloat16)
    rest = TEACH - S_DEV - EDGE
    grad_ref[S_DEV : TEACH - EDGE, :] = target[:rest, :].astype(jnp.bfloat16)
    for k in range(2):
        grad_copy(k).wait_recv()
    low = result[:EDGE, :] + jnp.concatenate([landed[0], jnp.zeros_like(landed[0])], axis=0)
    grad_ref[:EDGE, :] = low.astype(jnp.bfloat16)
    high = target[rest : rest + EDGE, :] + jnp.concatenate(
        [jnp.zeros_like(landed[1]), landed[1]], axis=0
    )
    grad_ref[TEACH - EDGE :, :] = high.astype(jnp.bfloat16)

    for k in range(2):
        edge_copy(k).wait_send()
        grad_copy(k).wait_send()
    for q in range(4):
        x_to_pair(tp, q).wait_send()
        x_to_right(tp, q).wait_send()
        x_to_left(tp, q).wait_send()
    for q in (2, 3):
        x_to_right(pair, q).wait_send()
        x_to_left(pair, q).wait_send()
    for slot, q in ((prev, 0), (prev, 2), (prev_other, 2)):
        x_to_right(slot, q).wait_send()
    for slot, q in ((nxt, 1), (nxt, 3), (nxt_other, 3)):
        x_to_left(slot, q).wait_send()
    for slot in (prev, nxt, far):
        for q in range(2):
            x_to_pair(slot, q).wait_send()
    def sent_own(kinds):
        for kind in kinds:
            for p in range(2):
                for hops in range(4 if p == 0 else 3):
                    to_right(kind, hops, p).wait_send()
                for hops in range(3 if p == 0 else 4):
                    to_left(kind, hops, p).wait_send()

    for_ring(sent_own)

    def sent(steps, _):
        slot = (z + steps) % N_Z * 2 + core
        for kind in range(2):
            to_sibling(kind, y_hi * 16 + slot).wait_send()

        @pl.when(y_hi == 0)
        def _():
            for p in range(2):
                to_cross(slot, p).wait_send()

        @pl.when((y_hi == 1) | (steps > 0))
        def _():
            for p in range(2):
                to_pair(slot, p).wait_send()

        @pl.when(y_hi == 1)
        def _():
            for kind in range(2):
                to_sibling(kind, slot).wait_send()

        return 0

    lax.fori_loop(0, N_Z, sent, 0)


def place_kernel(rows_ref, grad_in, out_ref, grad_ref, sems):
    copies = []
    for source, result, first in ((rows_ref, out_ref, 0), (grad_in, grad_ref, 4)):
        for k in range(4):
            size = source.shape[0] // 4
            part = pl.ds(k * size, size)
            copies.append(pltpu.make_async_copy(source.at[part], result.at[part], sems.at[first + k]))
    for one in copies:
        one.start()
    for one in copies:
        one.wait()


def body(student_rows, queries, keys_values, out_weight, teacher_rows, span_start, span_len):
    in_vmem, anywhere = pl.BlockSpec(memory_space=pltpu.VMEM), pl.BlockSpec(memory_space=pl.ANY)
    dma = pltpu.SemaphoreType.DMA
    bf16, f32 = jnp.bfloat16, jnp.float32
    wide = 4 * S_DEV
    results = (
        jax.ShapeDtypeStruct((S_DEV, WIDTH), bf16),
        jax.ShapeDtypeStruct((TEACH, WIDTH), bf16),
    )
    rows, grad = pl.pallas_call(
        layer_kernel,
        out_shape=results,
        in_specs=[anywhere] * 5 + [in_vmem] * 2,
        out_specs=(in_vmem, in_vmem),
        scratch_shapes=[
            pltpu.VMEM((2, 32 * S_DEV, HD), bf16),
            pltpu.VMEM((S_DEV, HD), bf16),
            pltpu.VMEM((S_DEV, DEPTH), bf16),
            pltpu.VMEM((HD, wide), bf16),
            pltpu.VMEM((2, 2 * S_DEV, wide // 2), f32),
            pltpu.VMEM((1, wide), f32),
            pltpu.VMEM((1, wide), f32),
            pltpu.VMEM((1, wide), f32),
            pltpu.VMEM((HD, wide), f32),
            pltpu.VMEM((8, S_DEV, DEPTH), bf16),
            pltpu.VMEM((8 * DEPTH, WIDTH), bf16),
            pltpu.VMEM((S_DEV, WIDTH), bf16),
            pltpu.VMEM((512, WIDTH), bf16),
            pltpu.VMEM((S_DEV, 512), bf16),
            pltpu.VMEM((WINDOW, S_DEV), bf16),
            pltpu.VMEM((S_DEV, WIDTH), f32),
            pltpu.VMEM((S_DEV, WIDTH), f32),
            pltpu.VMEM((S_DEV, HD), f32),
            pltpu.VMEM((2, HALO, WIDTH), f32),
            pltpu.VMEM((2, HALO, WIDTH), f32),
            dma((2, 64)), dma((2, 32)), dma((2, 8)), dma((2, 8)), dma((2, 32)), dma((16,)), dma((16,)),
            dma((8, 4)), dma((8, 4)), dma((8, 4)), dma((8, 4)), dma((5,)), dma((8,)), dma((4,)), dma((4,)),
        ],
        compiler_params=pltpu.CompilerParams(
            collective_id=0, has_side_effects=True, vmem_limit_bytes=60 << 20
        ),
        name="layer",
    )(
        queries, keys_values, student_rows, out_weight, teacher_rows,
        span_start.reshape(1, S_DEV), span_len.reshape(1, S_DEV),
    )
    return pl.pallas_call(
        place_kernel,
        out_shape=results,
        in_specs=[anywhere] * 2,
        out_specs=(anywhere, anywhere),
        scratch_shapes=[dma((8,))],
        compiler_params=pltpu.CompilerParams(vmem_limit_bytes=60 << 20),
        name="place",
    )(rows, grad)


def solution(mesh):
    return jax.shard_map(
        body,
        mesh=mesh,
        in_specs=(
            P("ctx", "tp"),
            P("ctx", "tp"),
            P(None, "ctx", None),
            P(None, "tp"),
            P("ctx", "tp"),
            P("ctx"),
            P("ctx"),
        ),
        out_specs=(P("ctx", "tp"), P("ctx", "tp")),
        check_vma=False,
    )
```

time: 101 us -> 107 us (1.059)
  the two profiles are of different devices: /device:TPU:16 before, /device:TPU:25 now
where the time goes in v3:
time: 107 us
  Pallas kernels  106 us (99%)
    pallas_call x1, Pallas kernels, body(): pl.pallas_call(layer_kernel, out_shape=results, in_specs=[anywhere] * 5 +...  65.6 us
    pallas_call x1, Pallas kernels, body(): pl.pallas_call(place_kernel, out_shape=results, in_specs=[anywhere] * 2,...  40.9 us

profile of v3, /device:TPU:25, one launch (start us, length us, event | category | flops | bytes accessed | tf_op | source)
XLA Modules:
  0.0 107.1 jit_solution(665084077282910525)
XLA Ops:
  0.6 65.6 %layer.1 = (bf16[256,1024]{1,0:T(8,128)(2,1)}, bf16[384,1024]{1,0:T(8,128)(2,1)}) custom-call(bf16[256,512]{1,0:T(8,128)(2,1)} %q_ref.1, bf16[2,256,512]{2,1,0:T(8,128)(2,1)} %kv_ref.1, bf16[256,1024]{1,0:T(8,128)(2,1)} %student_ref.1, bf16[4096,1024]{1,0:T(8,128)(2,1)} %weight_ref.1, bf16[384,1024]{1,0:T(8,128)(2,1)} %teacher_ref.1, s32[1,256]{1,0:T(1,128)} %bitcast.2, ...), custom_call_target="tpu_custom_call" | custom-call | tf_op jit(solution)/shard_map/layer/pallas_call | solution.py:550
  66.2 40.9 %place.1 = (bf16[256,1024]{1,0:T(8,128)(2,1)}, bf16[384,1024]{1,0:T(8,128)(2,1)}) custom-call(bf16[256,1024]{1,0:T(8,128)(2,1)} %get-tuple-element.4.rows_ref, bf16[384,1024]{1,0:T(8,128)(2,1)} %get-tuple-element.5.grad_in), custom_call_target="tpu_custom_call" | custom-call | tf_op jit(solution)/shard_map/place/pallas_call | solution.py:587

commit v4 on v3

--- a/solution.py
+++ b/solution.py
@@ -36,8 +36,7 @@
     q_ref, kv_ref, student_ref, weight_ref, teacher_ref, start_ref, len_ref, out_ref, grad_ref,
     buf, own_v, q_rows, q_t, scores, peak, decay, total, accum,
     att, weight, student, ext, member, member_t, result, target, counts, edges, landed,
-    recv, recv_sib, send_right, send_left, send_sib, send_cross, send_pair,
-    x_recv, x_send_right, x_send_left, x_send_pair, load, load_weight, edge_send, edge_recv,
+    starts, lens, recv, recv_sib, sent, x_recv, load, edge_recv,
 ):
     ctx, tp = lax.axis_index("ctx"), lax.axis_index("tp")
     core, z, y_hi = ctx % 2, (ctx // 2) % N_Z, ctx // 16
@@ -61,32 +60,39 @@
     def part(kind, slot):
         return buf.at[kind, pl.ds(pl.multiple_of(slot * S_DEV, S_DEV), S_DEV)]
 
-    def copy(kind, slot, p, to_ctx, to_tp, sem):
+    def copy(kind, slot, p, to_ctx, to_tp):
         return pltpu.make_async_remote_copy(
-            src_ref=piece(kind, slot, p), dst_ref=piece(kind, slot, p), send_sem=sem,
-            recv_sem=recv.at[kind, slot * 2 + p], device_id=(to_ctx, to_tp), device_id_type=MESH,
+            src_ref=piece(kind, slot, p), dst_ref=piece(kind, slot, p), send_sem=sent.at[0],
+            recv_sem=recv.at[kind, slot // 2 * 2 + p], device_id=(to_ctx, to_tp), device_id_type=MESH,
         )
 
     def arrived(kind, slot, p):
-        copy(kind, slot, p, ctx, pair, send_pair.at[0]).wait_recv()
+        copy(kind, slot, p, ctx, pair).wait_recv()
 
     def to_sibling(kind, slot):
         return pltpu.make_async_remote_copy(
-            src_ref=part(kind, slot), dst_ref=part(kind, slot), send_sem=send_sib.at[kind, slot],
-            recv_sem=recv_sib.at[kind, slot], device_id=(sibling, tp), device_id_type=MESH,
-        )
+            src_ref=part(kind, slot), dst_ref=part(kind, slot), send_sem=sent.at[0],
+            recv_sem=recv_sib.at[slot // 2], device_id=(sibling, tp), device_id_type=MESH,
+        )
+
+    def from_sibling(block):
+        both = buf.at[0, pl.ds(0, 2 * S_DEV)]
+        pltpu.make_async_remote_copy(
+            src_ref=both, dst_ref=both, send_sem=sent.at[0], recv_sem=recv_sib.at[block],
+            device_id=(sibling, tp), device_id_type=MESH,
+        ).wait_recv()
 
     def to_right(kind, hops, p):
-        return copy(kind, at(y_hi, -hops), p, right, tp, send_right.at[kind, hops * 2 + p])
+        return copy(kind, at(y_hi, -hops), p, right, tp)
 
     def to_left(kind, hops, p):
-        return copy(kind, at(y_hi, hops), p, left, tp, send_left.at[kind, hops * 2 + p])
+        return copy(kind, at(y_hi, hops), p, left, tp)
 
     def to_cross(slot, p):
-        return copy(y_lo, slot, p, other_hi, pair, send_cross.at[slot // 2 % N_Z * 2 + p])
+        return copy(y_lo, slot, p, other_hi, pair)
 
     def to_pair(slot, p):
-        return copy(kind_on, slot, p, ctx, pair, send_pair.at[slot // 2 % N_Z * 2 + p])
+        return copy(kind_on, slot, p, ctx, pair)
 
     k_load = pltpu.make_async_copy(
         kv_ref.at[0, :, pl.ds(pl.multiple_of(x * HD, HD), HD)], part(0, ctx), load.at[3]
@@ -95,9 +101,13 @@
         kv_ref.at[1, :, pl.ds(pl.multiple_of(x * HD, HD), HD)], own_v, load.at[0]
     )
     q_load = pltpu.make_async_copy(q_ref, q_rows, load.at[4])
+    start_load = pltpu.make_async_copy(start_ref, starts, load.at[6])
+    len_load = pltpu.make_async_copy(len_ref, lens, load.at[7])
     v_load.start()
     k_load.start()
     q_load.start()
+    start_load.start()
+    len_load.start()
     barrier = pltpu.get_barrier_semaphore()
     for to_ctx, to_tp in (
         (right, tp), (left, tp), (sibling, tp), (other_hi, pair), (ctx, pair),
@@ -191,15 +201,15 @@
     def quarter(slot, q):
         return att.at[slot, pl.ds(q * QUARTER, QUARTER)]
 
-    def send(slot, q, to_tp, sems):
+    def send(slot, q, to_tp):
         return pltpu.make_async_remote_copy(
-            src_ref=quarter(slot, q), dst_ref=quarter(slot, q), send_sem=sems.at[slot, q],
+            src_ref=quarter(slot, q), dst_ref=quarter(slot, q), send_sem=sent.at[0],
             recv_sem=x_recv.at[slot, q], device_id=(ctx, to_tp), device_id_type=MESH,
         )
 
-    x_to_right = lambda slot, q: send(slot, q, x_right, x_send_right)
-    x_to_left = lambda slot, q: send(slot, q, x_left, x_send_left)
-    x_to_pair = lambda slot, q: send(slot, q, pair, x_send_pair)
+    x_to_right = lambda slot, q: send(slot, q, x_right)
+    x_to_left = lambda slot, q: send(slot, q, x_left)
+    x_to_pair = lambda slot, q: send(slot, q, pair)
 
     def landed_at(slot, q):
         x_to_pair(slot, q).wait_recv()
@@ -209,20 +219,20 @@
         src = teacher_ref.at[pl.ds(TEACH - EDGE, EDGE)] if k == 0 else teacher_ref.at[pl.ds(0, EDGE)]
         dst = ext.at[pl.ds(0, EDGE)] if k == 0 else ext.at[pl.ds(EDGE + TEACH, EDGE)]
         return pltpu.make_async_remote_copy(
-            src_ref=src, dst_ref=dst, send_sem=edge_send.at[k], recv_sem=edge_recv.at[k],
+            src_ref=src, dst_ref=dst, send_sem=sent.at[0], recv_sem=edge_recv.at[k],
             device_id=(to_ctx, tp), device_id_type=MESH,
         )
 
     def grad_copy(k):
         return pltpu.make_async_remote_copy(
-            src_ref=edges.at[k], dst_ref=landed.at[k], send_sem=edge_send.at[2 + k],
+            src_ref=edges.at[k], dst_ref=landed.at[k], send_sem=sent.at[0],
             recv_sem=edge_recv.at[2 + k], device_id=(above if k == 0 else below, tp),
             device_id_type=MESH,
         )
 
     def weight_load(slot):
         rows = pl.ds(pl.multiple_of(slot * DEPTH, DEPTH), DEPTH)
-        return pltpu.make_async_copy(weight_ref.at[rows], weight.at[rows], load_weight.at[slot])
+        return pltpu.make_async_copy(weight_ref.at[rows], weight.at[rows], load.at[5])
 
     student_load = pltpu.make_async_copy(student_ref, student, load.at[1])
     teacher_load = pltpu.make_async_copy(teacher_ref, ext.at[pl.ds(EDGE, TEACH)], load.at[2])
@@ -231,11 +241,7 @@
             edge_copy(k).start()
         student_load.start()
         teacher_load.start()
-        order = [
-            tp, pair, slot_at(-1, True), slot_at(1, True), slot_at(2, True),
-            slot_at(-1, False), slot_at(1, False), slot_at(2, False),
-        ]
-        for slot in order:
+        for slot in range(8):
             weight_load(slot).start()
 
     half_rows = 2 * S_DEV
@@ -282,9 +288,7 @@
             accum[:, cols] = accum[:, cols] * shrink + product
 
     own_block = ctx // 2
-    edge_and_loads()
-    for kind in range(2):
-        to_sibling(kind, sibling).wait_recv()
+    from_sibling(ctx // 2)
     score(own_block, 0, masked=True)
     score(own_block, 1, masked=True)
     gather_values(own_block, 0, first=True)
@@ -327,13 +331,16 @@
                             else:
                                 action(hops)
 
+        @pl.when(n == 9)
+        def _():
+            edge_and_loads()
+
         block = jnp.where(plane == 2, block_z, y_hi * N_Z + block_z)
         here = plane > 0
 
         @pl.when(here)
         def _():
-            for kind in range(2):
-                to_sibling(kind, block * 2 + 1 - core).wait_recv()
+            from_sibling(block)
 
         def compute(prior):
             score(block, 0)
@@ -357,7 +364,9 @@
         x_to_left(tp, (1, 3, 0, 2)[k]).start()
     ext[WINDOW:, :] = jnp.zeros((ext.shape[0] - WINDOW, WIDTH), jnp.bfloat16)
     first = ctx * TEACH - EDGE
-    start_row, len_row = start_ref[...], len_ref[...]
+    start_load.wait()
+    len_load.wait()
+    start_row, len_row = starts[...], lens[...]
     row_pos = first + lax.broadcasted_iota(jnp.int32, (WINDOW, S_DEV), 0)
     inside = (row_pos >= start_row) & (row_pos < start_row + len_row)
     member_t[...] = jnp.where(inside, 1.0, 0.0).astype(jnp.bfloat16)
@@ -374,7 +383,6 @@
         return pl.ds(pl.multiple_of(j * TILE, TILE), TILE)
 
     def multiply(slot):
-        weight_load(slot).wait()
         rows = pl.ds(pl.multiple_of(slot * DEPTH, DEPTH), DEPTH)
 
         @pl.loop(0, WIDTH // TILE)
@@ -393,6 +401,7 @@
     landed_at(pair, 3)
     x_to_left(pair, 3).start()
     x_to_right(pair, 3).start()
+    pltpu.make_async_copy(weight_ref, weight, load.at[5]).wait()
     multiply(tp)
     landed_at(prev, 0)
     x_to_right(prev, 0).start()
@@ -443,7 +452,6 @@
     multiply(nxt_other)
     for q in (2, 3, 0, 1):
         landed_at(far_other, q)
-    weight_load(far_other).wait()
     last_rows = pl.ds(pl.multiple_of(far_other * DEPTH, DEPTH), DEPTH)
 
     @pl.loop(0, WIDTH // TILE)
@@ -451,7 +459,7 @@
         student32 = result[:, columns(j)] + jnp.dot(
             att[far_other], weight[last_rows, columns(j)], preferred_element_type=jnp.float32
         )
-        out_ref[:, columns(j)] = student32.astype(jnp.bfloat16)
+        student[:, columns(j)] = student32.astype(jnp.bfloat16)
         weighted = ((student32 - target[:, columns(j)]) * counts[:, :1]).astype(jnp.bfloat16)
         spread = jnp.dot(member_t[...], weighted, preferred_element_type=jnp.float32)
         edges[0, :, columns(j)] = spread[EDGE + TEACH : EDGE + TEACH + HALO]
@@ -461,85 +469,71 @@
 
     for k in range(2):
         grad_copy(k).start()
-    grad_ref[EDGE:S_DEV, :] = result[EDGE:, :].astype(jnp.bfloat16)
+    out_store = pltpu.make_async_copy(student, out_ref, load.at[0])
+    out_store.start()
+    ext[EDGE:S_DEV, :] = result[EDGE:, :].astype(jnp.bfloat16)
     rest = TEACH - S_DEV - EDGE
-    grad_ref[S_DEV : TEACH - EDGE, :] = target[:rest, :].astype(jnp.bfloat16)
+    ext[S_DEV : TEACH - EDGE, :] = target[:rest, :].astype(jnp.bfloat16)
+    grad_stores = [
+        pltpu.make_async_copy(ext.at[part], grad_ref.at[part], load.at[1 + k])
+        for k, part in enumerate(
+            (pl.ds(EDGE, TEACH - 2 * EDGE), pl.ds(0, EDGE), pl.ds(TEACH - EDGE, EDGE))
+        )
+    ]
+    grad_stores[0].start()
     for k in range(2):
         grad_copy(k).wait_recv()
     low = result[:EDGE, :] + jnp.concatenate([landed[0], jnp.zeros_like(landed[0])], axis=0)
-    grad_ref[:EDGE, :] = low.astype(jnp.bfloat16)
+    ext[:EDGE, :] = low.astype(jnp.bfloat16)
+    grad_stores[1].start()
     high = target[rest : rest + EDGE, :] + jnp.concatenate(
         [jnp.zeros_like(landed[1]), landed[1]], axis=0
     )
-    grad_ref[TEACH - EDGE :, :] = high.astype(jnp.bfloat16)
-
-    for k in range(2):
-        edge_copy(k).wait_send()
-        grad_copy(k).wait_send()
-    for q in range(4):
-        x_to_pair(tp, q).wait_send()
-        x_to_right(tp, q).wait_send()
-        x_to_left(tp, q).wait_send()
-    for q in (2, 3):
-        x_to_right(pair, q).wait_send()
-        x_to_left(pair, q).wait_send()
-    for slot, q in ((prev, 0), (prev, 2), (prev_other, 2)):
-        x_to_right(slot, q).wait_send()
-    for slot, q in ((nxt, 1), (nxt, 3), (nxt_other, 3)):
-        x_to_left(slot, q).wait_send()
-    for slot in (prev, nxt, far):
-        for q in range(2):
-            x_to_pair(slot, q).wait_send()
-    def sent_own(kinds):
-        for kind in kinds:
-            for p in range(2):
-                for hops in range(4 if p == 0 else 3):
-                    to_right(kind, hops, p).wait_send()
-                for hops in range(3 if p == 0 else 4):
-                    to_left(kind, hops, p).wait_send()
-
-    for_ring(sent_own)
-
-    def sent(steps, _):
-        slot = (z + steps) % N_Z * 2 + core
-        for kind in range(2):
-            to_sibling(kind, y_hi * 16 + slot).wait_send()
-
-        @pl.when(y_hi == 0)
-        def _():
-            for p in range(2):
-                to_cross(slot, p).wait_send()
-
-        @pl.when((y_hi == 1) | (steps > 0))
-        def _():
-            for p in range(2):
-                to_pair(slot, p).wait_send()
-
-        @pl.when(y_hi == 1)
-        def _():
-            for kind in range(2):
-                to_sibling(kind, slot).wait_send()
-
-        return 0
-
-    lax.fori_loop(0, N_Z, sent, 0)
-
-
-def place_kernel(rows_ref, grad_in, out_ref, grad_ref, sems):
-    copies = []
-    for source, result, first in ((rows_ref, out_ref, 0), (grad_in, grad_ref, 4)):
-        for k in range(4):
-            size = source.shape[0] // 4
+    ext[TEACH - EDGE : TEACH, :] = high.astype(jnp.bfloat16)
+    grad_stores[2].start()
+
+    out_store.wait()
+    for store in grad_stores:
+        store.wait()
+
+    def all_sent(pieces):
+        rows = weight.at[pl.ds(0, pieces * 16)]
+        pltpu.make_async_remote_copy(
+            src_ref=rows, dst_ref=rows, send_sem=sent.at[0], recv_sem=edge_recv.at[0],
+            device_id=(sibling, tp), device_id_type=MESH,
+        ).wait_send()
+
+    @pl.when(y_hi == 0)
+    def _():
+        all_sent(14 + 16 + 14 + 32 + 60)
+
+    @pl.when(y_hi == 1)
+    def _():
+        all_sent(28 + 16 + 64 + 60)
+
+
+def place_kernel(rows_in, grad_in, out_ref, grad_ref, rows, grad, sems):
+    pairs = []
+    for source, middle, result in ((rows_in, rows, out_ref), (grad_in, grad, grad_ref)):
+        for k in range(2):
+            size = source.shape[0] // 2
             part = pl.ds(k * size, size)
-            copies.append(pltpu.make_async_copy(source.at[part], result.at[part], sems.at[first + k]))
-    for one in copies:
-        one.start()
-    for one in copies:
-        one.wait()
+            at = len(pairs)
+            pairs.append((
+                pltpu.make_async_copy(source.at[part], middle.at[part], sems.at[0, at]),
+                pltpu.make_async_copy(middle.at[part], result.at[part], sems.at[1, at]),
+            ))
+    for fetch, _ in pairs:
+        fetch.start()
+    for fetch, store in pairs:
+        fetch.wait()
+        store.start()
+    for _, store in pairs:
+        store.wait()
 
 
 def body(student_rows, queries, keys_values, out_weight, teacher_rows, span_start, span_len):
-    in_vmem, anywhere = pl.BlockSpec(memory_space=pltpu.VMEM), pl.BlockSpec(memory_space=pl.ANY)
+    anywhere = pl.BlockSpec(memory_space=pl.ANY)
     dma = pltpu.SemaphoreType.DMA
     bf16, f32 = jnp.bfloat16, jnp.float32
     wide = 4 * S_DEV
@@ -550,8 +544,8 @@
     rows, grad = pl.pallas_call(
         layer_kernel,
         out_shape=results,
-        in_specs=[anywhere] * 5 + [in_vmem] * 2,
-        out_specs=(in_vmem, in_vmem),
+        in_specs=[anywhere] * 7,
+        out_specs=(anywhere, anywhere),
         scratch_shapes=[
             pltpu.VMEM((2, 32 * S_DEV, HD), bf16),
             pltpu.VMEM((S_DEV, HD), bf16),
@@ -573,8 +567,9 @@
             pltpu.VMEM((S_DEV, HD), f32),
             pltpu.VMEM((2, HALO, WIDTH), f32),
             pltpu.VMEM((2, HALO, WIDTH), f32),
-            dma((2, 64)), dma((2, 32)), dma((2, 8)), dma((2, 8)), dma((2, 32)), dma((16,)), dma((16,)),
-            dma((8, 4)), dma((8, 4)), dma((8, 4)), dma((8, 4)), dma((5,)), dma((8,)), dma((4,)), dma((4,)),
+            pltpu.VMEM((1, S_DEV), jnp.int32),
+            pltpu.VMEM((1, S_DEV), jnp.int32),
+            dma((2, 32)), dma((16,)), dma((1,)), dma((8, 4)), dma((8,)), dma((4,)),
         ],
         compiler_params=pltpu.CompilerParams(
             collective_id=0, has_side_effects=True, vmem_limit_bytes=60 << 20
@@ -589,7 +584,11 @@
         out_shape=results,
         in_specs=[anywhere] * 2,
         out_specs=(anywhere, anywhere),
-        scratch_shapes=[dma((8,))],
+        scratch_shapes=[
+            pltpu.VMEM((S_DEV, WIDTH), bf16),
+            pltpu.VMEM((TEACH, WIDTH), bf16),
+            dma((2, 4)),
+        ],
         compiler_params=pltpu.CompilerParams(vmem_limit_bytes=60 << 20),
         name="place",
     )(rows, grad)

time: 107 us -> 63.9 us (0.60)
  Pallas kernels: 106 us -> 63.2 us
    pallas_call x1, Pallas kernels: 40.9 us -> 2.1 us  [body(): pl.pallas_call(place_kernel, out_shape=results, in_specs=[anywhere] * 2,...]
    pallas_call x1, Pallas kernels: 65.6 us -> 61.1 us  [body(): pl.pallas_call(layer_kernel, out_shape=results, in_specs=[anywhere] * 7,...]
where the time goes in v4:
time: 63.9 us; the launch traced here: 63.8 us
  Pallas kernels  63.2 us (99%)
  between operations  0.64 us (1%)
    pallas_call x1, Pallas kernels, body(): pl.pallas_call(layer_kernel, out_shape=results, in_specs=[anywhere] * 7,...  61.1 us
    pallas_call x1, Pallas kernels, body(): pl.pallas_call(place_kernel, out_shape=results, in_specs=[anywhere] * 2,...  2.1 us

profile of v4, /device:TPU:25, one launch (start us, length us, event | category | flops | bytes accessed | tf_op | source)
XLA Modules:
  0.0 63.8 jit_solution(7998943620840680801)
XLA Ops:
  0.6 61.1 %layer.1 = (bf16[256,1024]{1,0:T(8,128)(2,1)}, bf16[384,1024]{1,0:T(8,128)(2,1)}) custom-call(bf16[256,512]{1,0:T(8,128)(2,1)} %q_ref.1, bf16[2,256,512]{2,1,0:T(8,128)(2,1)} %kv_ref.1, bf16[256,1024]{1,0:T(8,128)(2,1)} %student_ref.1, bf16[4096,1024]{1,0:T(8,128)(2,1)} %weight_ref.1, bf16[384,1024]{1,0:T(8,128)(2,1)} %teacher_ref.1, s32[1,256]{1,0:T(1,128)} %bitcast.2, ...), custom_call_target="tpu_custom_call" | custom-call | tf_op jit(solution)/shard_map/layer/pallas_call | solution.py:544
  61.7 2.1 %place.1 = (bf16[256,1024]{1,0:T(8,128)(2,1)}, bf16[384,1024]{1,0:T(8,128)(2,1)}) custom-call(bf16[256,1024]{1,0:T(8,128)(2,1)} %get-tuple-element.4.rows_in, bf16[384,1024]{1,0:T(8,128)(2,1)} %get-tuple-element.5.grad_in), custom_call_target="tpu_custom_call" | custom-call | tf_op jit(solution)/shard_map/place/pallas_call | solution.py:582

commit v5 on v4

--- a/solution.py
+++ b/solution.py
@@ -49,6 +49,7 @@
     kind_on = jnp.where(y_hi == 0, y_lo, 1 - y_lo)
     kind_swap = 1 - kind_on
     x_right, x_left = ((x + 1) % 4) * 2 + y_lo, ((x + 3) % 4) * 2 + y_lo
+    x_far = ((x + 2) % 4) * 2 + y_lo
     above, below = (ctx + 1) % 32, (ctx + 31) % 32
 
     def at(hi, steps):
@@ -87,6 +88,9 @@
 
     def to_left(kind, hops, p):
         return copy(kind, at(y_hi, hops), p, left, tp)
+
+    def to_second(slot, p, steps):
+        return copy(y_lo, slot, p, at(y_hi, steps), tp)
 
     def to_cross(slot, p):
         return copy(y_lo, slot, p, other_hi, pair)
@@ -111,7 +115,8 @@
     barrier = pltpu.get_barrier_semaphore()
     for to_ctx, to_tp in (
         (right, tp), (left, tp), (sibling, tp), (other_hi, pair), (ctx, pair),
-        (ctx, x_right), (ctx, x_left), (above, tp), (below, tp),
+        (ctx, x_right), (ctx, x_left), (ctx, x_far), (above, tp), (below, tp),
+        (at(y_hi, 2), tp), (at(y_hi, -2), tp),
     ):
         pl.semaphore_signal(barrier, inc=1, device_id=(to_ctx, to_tp), device_id_type=MESH)
     v_load.wait()
@@ -126,7 +131,7 @@
             q_rows[:, h * HD : (h + 1) * HD].astype(jnp.float32).T.astype(jnp.bfloat16)
         )
     k_load.wait()
-    pl.semaphore_wait(barrier, 9)
+    pl.semaphore_wait(barrier, 12)
 
     def for_ring(action):
         @pl.when(y_hi == 0)
@@ -138,28 +143,46 @@
             action([0, 1])
 
     def start_own(kinds):
+        if len(kinds) == 1:
+            for p in range(2):
+                to_second(ctx, p, 2).start()
+                to_second(ctx, 1 - p, -2).start()
+                to_cross(ctx, p).start()
         for p in range(2):
             for kind in kinds:
                 to_right(kind, 0, p).start()
                 to_left(kind, 0, 1 - p).start()
-            if len(kinds) == 1:
-                to_cross(ctx, p).start()
 
     for_ring(start_own)
     for kind in range(2):
         to_sibling(kind, ctx).start()
 
-    def ring(hops, kinds):
+    def low_ring(hops):
+        def side(sign, p):
+            slot = at(0, sign * hops)
+            arrived(y_lo, slot, p)
+            if hops == 2:
+                copy(y_lo, slot, p, left if sign > 0 else right, tp).start()
+                if (p == 0) == (sign < 0):
+                    to_second(slot, p, -2 * sign).start()
+            to_cross(slot, p).start()
+            to_pair(slot, p).start()
+
+        for p in range(2):
+            side(-1, p)
+            if hops < 4:
+                side(1, 1 - p)
+        for slot in low_slots(hops):
+            to_sibling(y_lo, slot).start()
+
+    def ring(hops):
         def side(kind, moving_right, p):
-            slot = at(y_hi, -hops if moving_right else hops)
-            arrived(kind, slot, p)
+            arrived(kind, at(y_hi, -hops if moving_right else hops), p)
             last = 3 if (p == 0) == moving_right else 2
             if hops <= last:
                 (to_right if moving_right else to_left)(kind, hops, p).start()
-            if len(kinds) == 1:
-                to_cross(slot, p).start()
-                to_pair(slot, p).start()
-
+
+        kinds = range(2)
         if hops < 4:
             for k in range(2):
                 for kind in kinds:
@@ -298,17 +321,17 @@
 
     low_order = {2: (1, -1), 3: (1, 1), 4: (1, -2), 5: (1, 2), 7: (1, -3), 8: (1, 3), 9: (1, 4)}
     low_events = {
-        1: [(ring, 1)], 2: [(from_pair, 1)], 3: [(ring, 2)], 4: [(from_pair, 2)], 5: [(ring, 3)],
-        6: [(ring, 4)], 7: [(from_pair, 3)], 8: [(from_pair, 4)],
+        1: [(low_ring, 2), (low_ring, 1), (low_ring, 3), (low_ring, 4)], 2: [(from_pair, 1)],
+        4: [(from_pair, 2)], 7: [(from_pair, 3)], 8: [(from_pair, 4)],
     }
     high_order = {
         1: (1, -1), 2: (1, 1), 3: (2, 0), 4: (1, -2), 5: (1, 2), 6: (2, -1), 7: (2, 1), 8: (1, -3),
-        9: (1, 3), 10: (1, 4), 11: (2, -2), 12: (2, 2), 13: (2, -3), 14: (2, 3), 15: (2, 4),
+        9: (1, 3), 10: (2, -2), 11: (2, 2), 12: (1, 4), 13: (2, -3), 14: (2, 3), 15: (2, 4),
     }
     high_events = {
-        1: [(ring, 1), (from_cross, 0)], 2: [(ring, 2), (from_cross, 1), (from_pair, 0)],
-        4: [(from_pair, 1)], 5: [(ring, 3), (from_cross, 2)], 7: [(from_pair, 2)],
-        8: [(ring, 4), (from_cross, 3)], 10: [(from_pair, 3), (from_cross, 4)], 12: [(from_pair, 4)],
+        1: [(ring, 1), (from_cross, 0)], 2: [(ring, 2), (from_pair, 0)],
+        3: [(from_cross, 1), (from_cross, 2)], 4: [(ring, 3)], 5: [(from_pair, 1), (from_pair, 2)],
+        6: [(from_cross, 3), (from_cross, 4)], 7: [(ring, 4)], 9: [(from_pair, 3), (from_pair, 4)],
     }
 
     def lookup(n, field):
@@ -319,17 +342,14 @@
     def step(n, before):
         plane = lookup(n, 0)
         block_z = (z + lookup(n, 1) + N_Z) % N_Z
-        for hi, events, kinds in ((0, low_events, [y_lo]), (1, high_events, [0, 1])):
+        for hi, events in ((0, low_events), (1, high_events)):
             @pl.when(y_hi == hi)
-            def _(events=events, kinds=kinds):
+            def _(events=events):
                 for k, todo in events.items():
                     @pl.when(n == k)
                     def _(todo=todo):
                         for action, hops in todo:
-                            if action is ring:
-                                ring(hops, kinds)
-                            else:
-                                action(hops)
+                            action(hops)
 
         @pl.when(n == 9)
         def _():
@@ -358,10 +378,11 @@
         att[tp, :, h * HD : (h + 1) * HD] = (accum[:, cols] / total[:, cols]).T.astype(jnp.bfloat16)
 
 
-    for k in range(4):
-        x_to_pair(tp, (2, 3, 0, 1)[k]).start()
-        x_to_right(tp, (0, 2, 1, 3)[k]).start()
-        x_to_left(tp, (1, 3, 0, 2)[k]).start()
+    for q in range(2):
+        x_to_right(tp, q).start()
+        x_to_left(tp, q).start()
+        x_to_pair(tp, 2 + q).start()
+        send(tp, q, x_far).start()
     ext[WINDOW:, :] = jnp.zeros((ext.shape[0] - WINDOW, WIDTH), jnp.bfloat16)
     first = ctx * TEACH - EDGE
     start_load.wait()
@@ -380,51 +401,44 @@
     result[...] = student[...].astype(jnp.float32)
 
     def columns(j):
-        return pl.ds(pl.multiple_of(j * TILE, TILE), TILE)
+        return pl.ds(j * TILE, TILE)
 
     def multiply(slot):
         rows = pl.ds(pl.multiple_of(slot * DEPTH, DEPTH), DEPTH)
 
-        @pl.loop(0, WIDTH // TILE)
-        def _(j):
-            result[:, columns(j)] += jnp.dot(
-                att[slot], weight[rows, columns(j)], preferred_element_type=jnp.float32
-            )
+        result[...] += jnp.dot(att[slot], weight[rows, :], preferred_element_type=jnp.float32)
 
     prev, nxt = slot_at(-1, True), slot_at(1, True)
     far, far_other = slot_at(2, True), slot_at(2, False)
     prev_other, nxt_other = slot_at(-1, False), slot_at(1, False)
 
-    landed_at(pair, 2)
-    x_to_right(pair, 2).start()
-    x_to_left(pair, 2).start()
-    landed_at(pair, 3)
-    x_to_left(pair, 3).start()
-    x_to_right(pair, 3).start()
+    for q in range(2):
+        x_to_right(tp, 2 + q).start()
+        x_to_left(tp, 2 + q).start()
+        x_to_pair(tp, q).start()
+    for q in (2, 3):
+        landed_at(pair, q)
+        x_to_right(pair, q).start()
+        x_to_left(pair, q).start()
     pltpu.make_async_copy(weight_ref, weight, load.at[5]).wait()
     multiply(tp)
-    landed_at(prev, 0)
-    x_to_right(prev, 0).start()
-    x_to_pair(prev, 0).start()
-    landed_at(nxt, 1)
-    x_to_left(nxt, 1).start()
-    x_to_pair(nxt, 1).start()
+    for q in range(2):
+        for slot in (prev, nxt):
+            landed_at(slot, q)
+            x_to_pair(slot, q).start()
     landed_at(prev, 2)
     x_to_right(prev, 2).start()
     landed_at(nxt, 3)
     x_to_left(nxt, 3).start()
-    landed_at(prev, 1)
-    x_to_pair(prev, 1).start()
-    landed_at(nxt, 0)
-    x_to_pair(nxt, 0).start()
+    for q in range(2):
+        landed_at(far, q)
+        x_to_pair(far, q).start()
     teacher_load.wait()
     for k in range(2):
         edge_copy(k).wait_recv()
 
-    @pl.loop(0, WIDTH // TILE)
-    def _(j):
-        summed = jnp.dot(member[...], ext[:, columns(j)], preferred_element_type=jnp.float32)
-        target[:, columns(j)] = summed * counts[:, :1]
+    summed = jnp.dot(member[...], ext[...], preferred_element_type=jnp.float32)
+    target[...] = summed * counts[:, :1]
 
     landed_at(pair, 0)
     landed_at(pair, 1)
@@ -433,10 +447,6 @@
     landed_at(nxt_other, 3)
     x_to_left(nxt_other, 3).start()
     multiply(pair)
-    landed_at(far, 0)
-    x_to_pair(far, 0).start()
-    landed_at(far, 1)
-    x_to_pair(far, 1).start()
     landed_at(prev, 3)
     multiply(prev)
     landed_at(nxt, 2)
@@ -454,8 +464,7 @@
         landed_at(far_other, q)
     last_rows = pl.ds(pl.multiple_of(far_other * DEPTH, DEPTH), DEPTH)
 
-    @pl.loop(0, WIDTH // TILE)
-    def _(j):
+    for j in range(WIDTH // TILE):
         student32 = result[:, columns(j)] + jnp.dot(
             att[far_other], weight[last_rows, columns(j)], preferred_element_type=jnp.float32
         )

time: 63.9 us -> 60.6 us (0.948)
  Pallas kernels: 63.2 us -> 59.8 us
    pallas_call x1, Pallas kernels: 61.1 us -> 57.7 us  [body(): pl.pallas_call(layer_kernel, out_shape=results, in_specs=[anywhere] * 7,...]
where the time goes in v5:
time: 60.6 us; the launch traced here: 60.5 us
  Pallas kernels  59.8 us (99%)
  between operations  0.64 us (1%)
    pallas_call x1, Pallas kernels, body(): pl.pallas_call(layer_kernel, out_shape=results, in_specs=[anywhere] * 7,...  57.7 us
    pallas_call x1, Pallas kernels, body(): pl.pallas_call(place_kernel, out_shape=results, in_specs=[anywhere] * 2,...  2.1 us

profile of v5, /device:TPU:25, one launch (start us, length us, event | category | flops | bytes accessed | tf_op | source)
XLA Modules:
  0.0 60.5 jit_solution(14026319297946610508)
XLA Ops:
  0.6 57.7 %layer.1 = (bf16[256,1024]{1,0:T(8,128)(2,1)}, bf16[384,1024]{1,0:T(8,128)(2,1)}) custom-call(bf16[256,512]{1,0:T(8,128)(2,1)} %q_ref.1, bf16[2,256,512]{2,1,0:T(8,128)(2,1)} %kv_ref.1, bf16[256,1024]{1,0:T(8,128)(2,1)} %student_ref.1, bf16[4096,1024]{1,0:T(8,128)(2,1)} %weight_ref.1, bf16[384,1024]{1,0:T(8,128)(2,1)} %teacher_ref.1, s32[1,256]{1,0:T(1,128)} %bitcast.2, ...), custom_call_target="tpu_custom_call" | custom-call | tf_op jit(solution)/shard_map/layer/pallas_call | solution.py:553
  58.4 2.1 %place.1 = (bf16[256,1024]{1,0:T(8,128)(2,1)}, bf16[384,1024]{1,0:T(8,128)(2,1)}) custom-call(bf16[256,1024]{1,0:T(8,128)(2,1)} %get-tuple-element.4.rows_in, bf16[384,1024]{1,0:T(8,128)(2,1)} %get-tuple-element.5.grad_in), custom_call_target="tpu_custom_call" | custom-call | tf_op jit(solution)/shard_map/place/pallas_call | solution.py:591

commit v6 on v5

--- a/solution.py
+++ b/solution.py
@@ -51,6 +51,7 @@
     x_right, x_left = ((x + 1) % 4) * 2 + y_lo, ((x + 3) % 4) * 2 + y_lo
     x_far = ((x + 2) % 4) * 2 + y_lo
     above, below = (ctx + 1) % 32, (ctx + 31) % 32
+    has_above, has_below = ctx < 31, ctx > 0
 
     def at(hi, steps):
         return hi * 16 + ((z + steps + N_Z) % N_Z) * 2 + core
@@ -115,47 +116,56 @@
     barrier = pltpu.get_barrier_semaphore()
     for to_ctx, to_tp in (
         (right, tp), (left, tp), (sibling, tp), (other_hi, pair), (ctx, pair),
-        (ctx, x_right), (ctx, x_left), (ctx, x_far), (above, tp), (below, tp),
+        (ctx, x_right), (ctx, x_left), (ctx, x_far),
         (at(y_hi, 2), tp), (at(y_hi, -2), tp),
     ):
         pl.semaphore_signal(barrier, inc=1, device_id=(to_ctx, to_tp), device_id_type=MESH)
+    for there, to_ctx in ((has_above, above), (has_below, below)):
+        @pl.when(there)
+        def _(to_ctx=to_ctx):
+            pl.semaphore_signal(barrier, inc=1, device_id=(to_ctx, tp), device_id_type=MESH)
+
     v_load.wait()
     v_own = own_v[...].astype(jnp.float32)
     for half in range(2):
         turned = v_own[half * HD : (half + 1) * HD].T.astype(jnp.bfloat16)
         start = pl.multiple_of(ctx * S_DEV + half * HD, HD)
         buf[1, pl.ds(start, HD), :] = turned
+    k_load.wait()
+    pl.semaphore_wait(barrier, jnp.where(has_above & has_below, 12, 11))
+
+    def start_near(kind):
+        for p in range(2):
+            to_right(kind, 0, p).start()
+            to_left(kind, 0, 1 - p).start()
+
+    @pl.when(y_hi == 0)
+    def _():
+        for p in range(2):
+            to_second(ctx, p, 2).start()
+            to_second(ctx, 1 - p, -2).start()
+            to_cross(ctx, p).start()
+
+    @pl.when(y_hi == 1)
+    def _():
+        start_near(0)
+
+    for kind in range(2):
+        to_sibling(kind, ctx).start()
+
     q_load.wait()
     for h in range(4):
         q_t[:, h * S_DEV : (h + 1) * S_DEV] = (
             q_rows[:, h * HD : (h + 1) * HD].astype(jnp.float32).T.astype(jnp.bfloat16)
         )
-    k_load.wait()
-    pl.semaphore_wait(barrier, 12)
-
-    def for_ring(action):
-        @pl.when(y_hi == 0)
-        def _():
-            action([y_lo])
-
-        @pl.when(y_hi == 1)
-        def _():
-            action([0, 1])
-
-    def start_own(kinds):
-        if len(kinds) == 1:
-            for p in range(2):
-                to_second(ctx, p, 2).start()
-                to_second(ctx, 1 - p, -2).start()
-                to_cross(ctx, p).start()
-        for p in range(2):
-            for kind in kinds:
-                to_right(kind, 0, p).start()
-                to_left(kind, 0, 1 - p).start()
-
-    for_ring(start_own)
-    for kind in range(2):
-        to_sibling(kind, ctx).start()
+
+    @pl.when(y_hi == 0)
+    def _():
+        start_near(y_lo)
+
+    @pl.when(y_hi == 1)
+    def _():
+        start_near(1)
 
     def low_ring(hops):
         def side(sign, p):
@@ -184,8 +194,8 @@
 
         kinds = range(2)
         if hops < 4:
-            for k in range(2):
-                for kind in kinds:
+            for kind in kinds:
+                for k in range(2):
                     side(kind, True, k)
                     side(kind, False, 1 - k)
             for kind in kinds:
@@ -246,10 +256,11 @@
             device_id=(to_ctx, tp), device_id_type=MESH,
         )
 
-    def grad_copy(k):
+    def grad_copy(k, half):
+        part = pl.ds(half * (WIDTH // 2), WIDTH // 2)
         return pltpu.make_async_remote_copy(
-            src_ref=edges.at[k], dst_ref=landed.at[k], send_sem=sent.at[0],
-            recv_sem=edge_recv.at[2 + k], device_id=(above if k == 0 else below, tp),
+            src_ref=edges.at[k, :, part], dst_ref=landed.at[k, :, part], send_sem=sent.at[0],
+            recv_sem=edge_recv.at[2 + 2 * k + half], device_id=(above if k == 0 else below, tp),
             device_id_type=MESH,
         )
 
@@ -260,8 +271,11 @@
     student_load = pltpu.make_async_copy(student_ref, student, load.at[1])
     teacher_load = pltpu.make_async_copy(teacher_ref, ext.at[pl.ds(EDGE, TEACH)], load.at[2])
     def edge_and_loads():
-        for k in range(2):
-            edge_copy(k).start()
+        for k, there in ((0, has_above), (1, has_below)):
+            @pl.when(there)
+            def _(k=k):
+                edge_copy(k).start()
+
         student_load.start()
         teacher_load.start()
         for slot in range(8):
@@ -325,13 +339,14 @@
         4: [(from_pair, 2)], 7: [(from_pair, 3)], 8: [(from_pair, 4)],
     }
     high_order = {
-        1: (1, -1), 2: (1, 1), 3: (2, 0), 4: (1, -2), 5: (1, 2), 6: (2, -1), 7: (2, 1), 8: (1, -3),
-        9: (1, 3), 10: (2, -2), 11: (2, 2), 12: (1, 4), 13: (2, -3), 14: (2, 3), 15: (2, 4),
+        1: (1, -1), 2: (1, 1), 3: (2, 0), 4: (1, -2), 5: (1, 2), 6: (1, -3), 7: (1, 3), 8: (2, -1),
+        9: (2, 1), 10: (2, -2), 11: (2, 2), 12: (1, 4), 13: (2, -3), 14: (2, 3), 15: (2, 4),
     }
     high_events = {
-        1: [(ring, 1), (from_cross, 0)], 2: [(ring, 2), (from_pair, 0)],
-        3: [(from_cross, 1), (from_cross, 2)], 4: [(ring, 3)], 5: [(from_pair, 1), (from_pair, 2)],
-        6: [(from_cross, 3), (from_cross, 4)], 7: [(ring, 4)], 9: [(from_pair, 3), (from_pair, 4)],
+        1: [(ring, 1), (from_cross, 0)], 3: [(ring, 2), (from_pair, 0)],
+        4: [(from_cross, 1), (from_cross, 2)], 6: [(ring, 3)], 7: [(from_cross, 3)],
+        8: [(from_cross, 4), (from_pair, 1), (from_pair, 2)], 11: [(ring, 4)],
+        12: [(from_pair, 3)], 13: [(from_pair, 4)],
     }
 
     def lookup(n, field):
@@ -382,7 +397,16 @@
         x_to_right(tp, q).start()
         x_to_left(tp, q).start()
         x_to_pair(tp, 2 + q).start()
-        send(tp, q, x_far).start()
+    @pl.when(ctx == 0)
+    def _():
+        ext[:EDGE, :] = jnp.zeros((EDGE, WIDTH), jnp.bfloat16)
+        landed[0] = jnp.zeros((HALO, WIDTH), jnp.float32)
+
+    @pl.when(ctx == 31)
+    def _():
+        ext[EDGE + TEACH : WINDOW, :] = jnp.zeros((EDGE, WIDTH), jnp.bfloat16)
+        landed[1] = jnp.zeros((HALO, WIDTH), jnp.float32)
+
     ext[WINDOW:, :] = jnp.zeros((ext.shape[0] - WINDOW, WIDTH), jnp.bfloat16)
     first = ctx * TEACH - EDGE
     start_load.wait()
@@ -391,6 +415,9 @@
     row_pos = first + lax.broadcasted_iota(jnp.int32, (WINDOW, S_DEV), 0)
     inside = (row_pos >= start_row) & (row_pos < start_row + len_row)
     member_t[...] = jnp.where(inside, 1.0, 0.0).astype(jnp.bfloat16)
+    for q in range(2):
+        send(tp, q, x_far).start()
+        x_to_pair(tp, q).start()
     wide_start = jnp.broadcast_to(start_row.astype(jnp.float32), (HD, S_DEV)).T[:, :1]
     wide_len = jnp.broadcast_to(len_row.astype(jnp.float32), (HD, S_DEV)).T
     counts[...] = 1.0 / wide_len
@@ -415,7 +442,6 @@
     for q in range(2):
         x_to_right(tp, 2 + q).start()
         x_to_left(tp, 2 + q).start()
-        x_to_pair(tp, q).start()
     for q in (2, 3):
         landed_at(pair, q)
         x_to_right(pair, q).start()
@@ -434,8 +460,11 @@
         landed_at(far, q)
         x_to_pair(far, q).start()
     teacher_load.wait()
-    for k in range(2):
-        edge_copy(k).wait_recv()
+    for k, there in ((0, has_below), (1, has_above)):
+        @pl.when(there)
+        def _(k=k):
+            edge_copy(k).wait_recv()
+
 
     summed = jnp.dot(member[...], ext[...], preferred_element_type=jnp.float32)
     target[...] = summed * counts[:, :1]
@@ -475,9 +504,13 @@
         edges[1, :, columns(j)] = spread[EDGE - HALO : EDGE]
         result[:, columns(j)] = spread[EDGE : EDGE + S_DEV]
         target[: TEACH - S_DEV, columns(j)] = spread[EDGE + S_DEV : EDGE + TEACH]
-
-    for k in range(2):
-        grad_copy(k).start()
+        if j % 2 == 1:
+            for k, there in ((0, has_above), (1, has_below)):
+                @pl.when(there)
+                def _(k=k, j=j):
+                    grad_copy(k, j // 2).start()
+
+
     out_store = pltpu.make_async_copy(student, out_ref, load.at[0])
     out_store.start()
     ext[EDGE:S_DEV, :] = result[EDGE:, :].astype(jnp.bfloat16)
@@ -490,8 +523,12 @@
         )
     ]
     grad_stores[0].start()
-    for k in range(2):
-        grad_copy(k).wait_recv()
+    for k, there in ((0, has_below), (1, has_above)):
+        @pl.when(there)
+        def _(k=k):
+            for half in range(2):
+                grad_copy(k, half).wait_recv()
+
     low = result[:EDGE, :] + jnp.concatenate([landed[0], jnp.zeros_like(landed[0])], axis=0)
     ext[:EDGE, :] = low.astype(jnp.bfloat16)
     grad_stores[1].start()
@@ -512,13 +549,16 @@
             device_id=(sibling, tp), device_id_type=MESH,
         ).wait_send()
 
-    @pl.when(y_hi == 0)
-    def _():
-        all_sent(14 + 16 + 14 + 32 + 60)
-
-    @pl.when(y_hi == 1)
-    def _():
-        all_sent(28 + 16 + 64 + 60)
+    for hi, pieces in ((0, 14 + 16 + 14 + 32 + 56), (1, 28 + 16 + 64 + 56)):
+        inner = has_above & has_below
+
+        @pl.when((y_hi == hi) & inner)
+        def _(pieces=pieces):
+            all_sent(pieces + 4)
+
+        @pl.when((y_hi == hi) & ~inner)
+        def _(pieces=pieces):
+            all_sent(pieces + 2)
 
 
 def place_kernel(rows_in, grad_in, out_ref, grad_ref, rows, grad, sems):
@@ -578,7 +618,7 @@
             pltpu.VMEM((2, HALO, WIDTH), f32),
             pltpu.VMEM((1, S_DEV), jnp.int32),
             pltpu.VMEM((1, S_DEV), jnp.int32),
-            dma((2, 32)), dma((16,)), dma((1,)), dma((8, 4)), dma((8,)), dma((4,)),
+            dma((2, 32)), dma((16,)), dma((1,)), dma((8, 4)), dma((8,)), dma((6,)),
         ],
         compiler_params=pltpu.CompilerParams(
             collective_id=0, has_side_effects=True, vmem_limit_bytes=60 << 20

time: 60.6 us -> 59.6 us (0.983); the launches traced: 60.5 us -> 58.8 us
  Pallas kernels: 59.8 us -> 58.2 us
    pallas_call x1, Pallas kernels: 57.7 us -> 56.1 us  [body(): pl.pallas_call(layer_kernel, out_shape=results, in_specs=[anywhere] * 7,...]
where the time goes in v6:
time: 59.6 us; the launch traced here: 58.8 us
  Pallas kernels  58.2 us (98%)
  between operations  0.64 us (1%)
    pallas_call x1, Pallas kernels, body(): pl.pallas_call(layer_kernel, out_shape=results, in_specs=[anywhere] * 7,...  56.1 us
    pallas_call x1, Pallas kernels, body(): pl.pallas_call(place_kernel, out_shape=results, in_specs=[anywhere] * 2,...  2.1 us

profile of v6, /device:TPU:25, one launch (start us, length us, event | category | flops | bytes accessed | tf_op | source)
XLA Modules:
  0.0 58.8 jit_solution(1000414182600093951)
XLA Ops:
  0.6 56.1 %layer.1 = (bf16[256,1024]{1,0:T(8,128)(2,1)}, bf16[384,1024]{1,0:T(8,128)(2,1)}) custom-call(bf16[256,512]{1,0:T(8,128)(2,1)} %q_ref.1, bf16[2,256,512]{2,1,0:T(8,128)(2,1)} %kv_ref.1, bf16[256,1024]{1,0:T(8,128)(2,1)} %student_ref.1, bf16[4096,1024]{1,0:T(8,128)(2,1)} %weight_ref.1, bf16[384,1024]{1,0:T(8,128)(2,1)} %teacher_ref.1, s32[1,256]{1,0:T(1,128)} %bitcast.2, ...), custom_call_target="tpu_custom_call" | custom-call | tf_op jit(solution)/shard_map/layer/pallas_call | solution.py:593
  56.7 2.1 %place.1 = (bf16[256,1024]{1,0:T(8,128)(2,1)}, bf16[384,1024]{1,0:T(8,128)(2,1)}) custom-call(bf16[256,1024]{1,0:T(8,128)(2,1)} %get-tuple-element.4.rows_in, bf16[384,1024]{1,0:T(8,128)(2,1)} %get-tuple-element.5.grad_in), custom_call_target="tpu_custom_call" | custom-call | tf_op jit(solution)/shard_map/place/pallas_call | solution.py:631

commit v7 on v6

--- a/solution.py
+++ b/solution.py
@@ -387,10 +387,15 @@
         return lax.cond(here & (block < own_block), compute, lambda prior: prior, before)
 
     last_block = lax.fori_loop(1, 16, step, own_block)
-    gather_values(last_block, 1)
-    for h in range(4):
+    def place_head(h):
         cols = slice(h * S_DEV, (h + 1) * S_DEV)
         att[tp, :, h * HD : (h + 1) * HD] = (accum[:, cols] / total[:, cols]).T.astype(jnp.bfloat16)
+
+    place_head(0)
+    place_head(1)
+    gather_values(last_block, 1)
+    place_head(2)
+    place_head(3)
 
 
     for q in range(2):

time: 59.6 us -> 59.6 us (level)
  no operation moved by 1% of the time
where the time goes in v7:
time: 59.6 us; the launch traced here: 58.8 us
  Pallas kernels  58.2 us (98%)
  between operations  0.64 us (1%)
    pallas_call x1, Pallas kernels, body(): pl.pallas_call(layer_kernel, out_shape=results, in_specs=[anywhere] * 7,...  56.1 us
    pallas_call x1, Pallas kernels, body(): pl.pallas_call(place_kernel, out_shape=results, in_specs=[anywhere] * 2,...  2.1 us

profile of v7, /device:TPU:25, one launch (start us, length us, event | category | flops | bytes accessed | tf_op | source)
XLA Modules:
  0.0 58.8 jit_solution(7954217149775664310)
XLA Ops:
  0.6 56.1 %layer.1 = (bf16[256,1024]{1,0:T(8,128)(2,1)}, bf16[384,1024]{1,0:T(8,128)(2,1)}) custom-call(bf16[256,512]{1,0:T(8,128)(2,1)} %q_ref.1, bf16[2,256,512]{2,1,0:T(8,128)(2,1)} %kv_ref.1, bf16[256,1024]{1,0:T(8,128)(2,1)} %student_ref.1, bf16[4096,1024]{1,0:T(8,128)(2,1)} %weight_ref.1, bf16[384,1024]{1,0:T(8,128)(2,1)} %teacher_ref.1, s32[1,256]{1,0:T(1,128)} %bitcast.2, ...), custom_call_target="tpu_custom_call" | custom-call | tf_op jit(solution)/shard_map/layer/pallas_call | solution.py:598
  56.7 2.1 %place.1 = (bf16[256,1024]{1,0:T(8,128)(2,1)}, bf16[384,1024]{1,0:T(8,128)(2,1)}) custom-call(bf16[256,1024]{1,0:T(8,128)(2,1)} %get-tuple-element.4.rows_in, bf16[384,1024]{1,0:T(8,128)(2,1)} %get-tuple-element.5.grad_in), custom_call_target="tpu_custom_call" | custom-call | tf_op jit(solution)/shard_map/place/pallas_call | solution.py:636
